TPU v7x, 32 devices: a whole 2x2x4 slice. The times are simulated.
32 devices in a mesh: dom: 4 (over y, core), fsdp: 8 (over z, x).
Axes of the slice: x: 2, y: 2, z: 4, core: 2. Of those that a mesh axis runs over, the one named last changes fastest.
Arguments:
- tokens: bfloat16 [8192, 1536], P(('dom', 'fsdp')), may hold values from -6 to 6
- gain: bfloat16 [1536], P('fsdp'), may hold values from 0.099609375 to 1.8984375
- kv_weight: bfloat16 [1536, 512], P('fsdp'), may hold values from -0.15625 to 0.15625
- positions: int32 [8192], P(('dom', 'fsdp')), may hold values from 0 to 4095
- cotangent: bfloat16 [8192, 512], P(('dom', 'fsdp')), may hold values from -6 to 6
- counts: int32 [4, 8], replicated, may hold values from 0 to 2, as said below
- ratios: int32 [4], replicated, may hold values from 1 to 8
Outputs:
- keys_values: bfloat16 [8192, 512], P(('dom', 'fsdp'))
- weight_grad: float32 [1536, 512], P('fsdp')
- gain_grad: float32 [1536], P('fsdp')
Inputs may be any that keep to these rules, and one draw needn't show every extreme that they name: counts gives each device's live rows in blocks of 128; every domain has a device with one or more live blocks, and some device holds 2 live blocks in every draw.
All inputs are finite; a program needn't handle non-finite values.
Results may differ from a plain program's by a relative error of at most 0.0051.
Values may be sent and summed in bfloat16 or wider, within the bound.
No kernel may reach another device: no remote copies, remote signals or barrier semaphores. Data moves between devices by JAX's collectives and lax.ppermute only.
A program may use at most 64 MiB of HBM per device.

v0:
```python
import functools

import jax
import jax.numpy as jnp
import numpy as np
from jax import lax
from jax.experimental import pallas as pl
from jax.experimental.pallas import tpu as pltpu
from jax.sharding import Mesh
from jax.sharding import PartitionSpec as P

KVH = 2
HD = 128
BLOCK = 128
CHUNK = 384
EVERY = ("outer", "core", "fsdp")
VMEM_BYTES = 32 * 1024 * 1024


def to_column(line):
    n = line.shape[1]
    rows = lax.broadcasted_iota(jnp.int32, (n, n), 0)
    lanes = lax.broadcasted_iota(jnp.int32, (n, n), 1)
    spread = jnp.broadcast_to(line, (n, n))
    return jnp.sum(jnp.where(rows == lanes, spread, 0.0), axis=1, keepdims=True)


def to_line(column):
    n = column.shape[0]
    rows = lax.broadcasted_iota(jnp.int32, (n, n), 0)
    lanes = lax.broadcasted_iota(jnp.int32, (n, n), 1)
    spread = jnp.broadcast_to(column, (n, n))
    return jnp.sum(jnp.where(rows == lanes, spread, 0.0), axis=0, keepdims=True)


def sine_cosine(angles):
    turns = jnp.floor(angles * (2.0 / np.pi) + 0.5)
    rest = angles - turns * 1.5703125
    rest = rest - turns * 4.837512969970703125e-4
    rest = rest - turns * 7.54978995489188216e-8
    square = rest * rest
    sine = (-1.9515295891e-4 * square + 8.3321608736e-3) * square - 1.6666654611e-1
    sine = sine * square * rest + rest
    cosine = (2.443315711809948e-5 * square - 1.388731625493765e-3) * square
    cosine = (cosine + 4.166664568298827e-2) * square * square - 0.5 * square + 1.0
    quarter = turns.astype(jnp.int32) & 3
    odd = (quarter & 1) == 1
    sines, cosines = jnp.where(odd, cosine, sine), jnp.where(odd, sine, cosine)
    sines = jnp.where(quarter >= 2, -sines, sines)
    cosines = jnp.where(((quarter + 1) & 2) == 2, -cosines, cosines)
    return sines, cosines


def transposed_dot(left, right):
    return lax.dot_general(
        left, right, (((0,), (0,)), ((), ())), preferred_element_type=jnp.float32
    )


def full_sum(values):
    return jnp.sum(jnp.sum(values, axis=1, keepdims=True), axis=0, keepdims=True)


def fetch(sources, buffers, semaphores):
    copies = []
    for i, (source, buffer) in enumerate(zip(sources, buffers)):
        copy = pltpu.make_async_copy(source, buffer, semaphores.at[i])
        copy.start()
        copies.append(copy)
    return copies


def call(kernel, out_shape, args, after=None, in_hbm=False, fetched=0, scratch=(), flops=0):
    count = len(args)
    args = [
        pltpu.with_memory_space_constraint(arg, pltpu.HBM) if i < fetched else arg
        for i, arg in enumerate(args)
    ]
    spaces = [pl.ANY] * fetched + [pltpu.VMEM] * (count - fetched)
    run = kernel
    if after is not None:
        if in_hbm:
            after = pltpu.with_memory_space_constraint(after, pltpu.HBM)
        args, spaces = args + [after], spaces + [pl.ANY]

        def run(*refs):
            kernel(*refs[:count], *refs[count + 1 :])

    scratch = list(scratch) + [pltpu.VMEM(arg.shape, arg.dtype) for arg in args[:fetched]]
    if fetched:
        scratch.append(pltpu.SemaphoreType.DMA((fetched,)))
    return pl.pallas_call(
        run,
        out_shape=out_shape,
        in_specs=[pl.BlockSpec(memory_space=space) for space in spaces],
        scratch_shapes=scratch,
        out_specs=jax.tree.map(lambda _: pl.BlockSpec(memory_space=pltpu.VMEM), out_shape),
        compiler_params=pltpu.CompilerParams(vmem_limit_bytes=VMEM_BYTES),
        cost_estimate=pl.CostEstimate(
            flops=flops, bytes_accessed=1000000, transcendentals=0
        ),
    )(*args)


def stack_kernel(*refs):
    for i, part_ref in enumerate(refs[:-1]):
        refs[-1][i] = part_ref[...]


def bundle_kernel(shifts, mine_ref, *refs):
    out_ref = refs[-1]
    rows = refs[0].shape[1]
    member = lax.axis_index("fsdp")
    parts = [part_ref.at[i] for part_ref in refs[:-1] for i in range(part_ref.shape[0])]
    for shift, part_ref in zip(shifts, parts):
        out_ref[aligned(jnp.bitwise_xor(member, shift), rows), :] = part_ref[...]
    out_ref[len(parts) * rows :, :] = mine_ref[...]


def backward_kernel(
    positions_hbm, frequency_hbm, counts_hbm, ratios_hbm, cotangent_hbm, tokens_hbm,
    gain_hbm, weight_hbm,
    normed_ref, cosines_ref, sines_ref, both_ref, given_ref, folded_ref,
    positions_ref, frequency_ref, counts_ref, ratios_ref, cotangent_ref, tokens_ref,
    gain_ref, weight_ref,
    semaphores,
):
    copies = fetch(
        (
            positions_hbm, frequency_hbm, counts_hbm, ratios_hbm, cotangent_hbm, tokens_hbm,
            gain_hbm, weight_hbm,
        ),
        (
            positions_ref, frequency_ref, counts_ref, ratios_ref, cotangent_ref, tokens_ref,
            gain_ref, weight_ref,
        ),
        semaphores,
    )
    rows, width = tokens_ref.shape
    core = lax.axis_index("core")
    domain = lax.axis_index("outer") * 2 + core
    member = lax.axis_index("fsdp")

    for copy in copies[:5]:
        copy.wait()
    lines = positions_ref[...].astype(jnp.float32)
    lanes = lax.broadcasted_iota(jnp.int32, (lines.shape[1], HD), 1)
    left = lanes < HD // 2
    first, second = to_column(lines[0:1, :]), to_column(lines[1:2, :])
    sines, cosines = sine_cosine(jnp.where(left, first, second) * frequency_ref[...])
    turned_sines, turned_cosines = pltpu.roll(sines, HD // 2, 1), pltpu.roll(cosines, HD // 2, 1)
    cosines = jnp.concatenate(
        [jnp.where(left, cosines, turned_cosines), jnp.where(left, turned_cosines, cosines)]
    )
    sines = jnp.concatenate(
        [jnp.where(left, -sines, turned_sines), jnp.where(left, -turned_sines, sines)]
    )
    cosines_ref[...] = cosines
    sines_ref[...] = sines

    counts = counts_ref[...].astype(jnp.float32)
    ratios = ratios_ref[...].astype(jnp.float32)
    at_domain = lax.broadcasted_iota(jnp.int32, counts.shape, 0) == domain
    at_member = lax.broadcasted_iota(jnp.int32, counts.shape, 1) == member
    ratio_at = lax.broadcasted_iota(jnp.int32, ratios.shape, 1) == domain
    live_total = full_sum(counts) * float(BLOCK)
    own_rows = full_sum(jnp.where(at_domain, counts, 0.0)) * float(BLOCK)
    own_live = full_sum(jnp.where(at_domain & at_member, counts, 0.0)) * float(BLOCK)
    own_ratio = full_sum(jnp.where(ratio_at, ratios, 0.0))
    factor = own_ratio / full_sum(ratios) * live_total / own_rows
    row_ids = lax.broadcasted_iota(jnp.int32, (rows, 1), 0).astype(jnp.float32)
    row_factor = jnp.where(row_ids < own_live, factor, 0.0)

    weighted = cotangent_ref[...].astype(jnp.float32) * row_factor
    key_width = KVH * HD
    turned = []
    for head in range(KVH):
        part = weighted[:, head * HD : (head + 1) * HD]
        turned.append(part * cosines - pltpu.roll(part, HD // 2, 1) * sines)
    keys = jnp.concatenate(turned, axis=1).astype(jnp.bfloat16)
    values = weighted[:, key_width:].astype(jnp.bfloat16)
    keep = jnp.where(core == 0, keys, values)
    give = jnp.where(core == 0, values, keys)
    half = keep.shape[1]
    both_ref[:, :half] = keep
    both_ref[:, half:] = give

    copies[5].wait()
    step = 32
    for start in range(0, rows, step):
        block = tokens_ref[start : start + step, :].astype(jnp.float32)
        mean_square = jnp.sum(block * block, axis=1, keepdims=True) * (1.0 / width)
        normed_ref[start : start + step, :] = (
            block * lax.rsqrt(mean_square + 1e-06)
        ).astype(jnp.bfloat16)

    for start in range(0, given_ref.shape[0], CHUNK):
        at = slice(start, start + CHUNK)
        given_ref[at, :] = transposed_dot(normed_ref[:, at], give).astype(jnp.bfloat16)

    columns = pl.ds(pl.multiple_of(core * half, half), half)
    copies[6].wait()
    gains = to_column(gain_ref[...].astype(jnp.float32).reshape(1, -1))
    copies[7].wait()
    folded = weight_ref[:, columns].astype(jnp.float32) * gains
    folded_ref[...] = folded.astype(jnp.bfloat16)


def rest_kernel(normed_ref, both_ref, own_ref, given_ref):
    width, half = own_ref.shape
    done = width - given_ref.shape[0]
    keep, both = both_ref[:, :half], both_ref[...]
    for start in range(0, width, CHUNK):
        at = slice(start, start + CHUNK)
        if start < done:
            own_ref[at, :] = transposed_dot(normed_ref[:, at], keep)
            continue
        result = transposed_dot(normed_ref[:, at], both)
        own_ref[at, :] = result[:, :half]
        given_ref[start - done : start - done + CHUNK, :] = result[:, half:].astype(jnp.bfloat16)


def aligned(index, size):
    return pl.ds(pl.multiple_of(index * size, size), size)


def total(kept, taken):
    return kept + taken.astype(jnp.float32)


def pair_kernel(own_ref, first_ref, second_ref, *out_refs):
    count, rows, _ = out_refs[0].shape
    first_count = first_ref.shape[0] // (4 * rows)
    y, x = lax.axis_index("outer"), lax.axis_index("fsdp") % 2
    for (away_y, away_x), out_ref in zip(((0, 0), (1, 1), (0, 1), (1, 0)), out_refs):
        to_y, to_x = jnp.bitwise_xor(y, away_y), jnp.bitwise_xor(x, away_x)
        for i in range(count):
            at = aligned(4 * i + 2 * to_x + to_y, rows)
            in_first = i < first_count
            taken_ref = first_ref if in_first else second_ref
            taken_at = 4 * (i if in_first else i - first_count) + 2 * to_x + to_y
            taken_at = aligned(taken_at, rows)
            out_ref[i] = total(own_ref[at, :], taken_ref[taken_at, :]).astype(out_ref.dtype)


def z_kernel(kept_ref, first_ref, second_ref, third_ref, *out_refs):
    z = lax.axis_index("fsdp") // 2
    for shift, out_ref in enumerate(out_refs):
        at = jnp.bitwise_xor(z, shift)
        result = total(kept_ref[at], first_ref[at])
        result = total(total(result, second_ref[at]), third_ref[at])
        out_ref[...] = result.astype(out_ref.dtype)


def last_kernel(own_ref, *refs):
    result = own_ref[...]
    for taken_ref in refs[:-1]:
        result = total(result, taken_ref[...])
    refs[-1][...] = result.astype(jnp.bfloat16)


def finish_kernel(counts_ref, gain_ref, weight_ref, *refs):
    parts, (weight_grad_ref, gain_grad_ref, sum_ref) = refs[:-3], refs[-3:]
    rows, half = parts[0].shape
    y, core = lax.axis_index("outer"), lax.axis_index("core")
    live_total = full_sum(counts_ref[...].astype(jnp.float32)) * float(BLOCK)
    scale = 1.0 / jnp.sqrt(live_total)
    gains = to_column(gain_ref[...].astype(jnp.float32).reshape(1, -1)) * scale
    shifts = (0, 1) if len(parts) == 2 else (0, 1, 2, 3)
    for shift, part_ref in zip(shifts, parts):
        at_y = 0 if len(parts) == 2 else jnp.bitwise_xor(y, shift // 2)
        at = jnp.bitwise_xor(core, shift % 2)
        tail = slice(part_ref.shape[0] - rows, None)
        sum_ref[aligned(at_y, rows), aligned(at, half)] = part_ref[tail, :].astype(jnp.float32)
    result = sum_ref[...]
    weight_grad_ref[...] = result * gains
    dots = jnp.sum(result * weight_ref[...].astype(jnp.float32), axis=1, keepdims=True)
    gain_grad_ref[...] = to_line(dots * scale).reshape(-1)


def forward_kernel(normed_ref, own_ref, other_ref, cosines_ref, sines_ref, out_ref):
    core = lax.axis_index("core")
    normed = normed_ref[...]
    width = normed.shape[1]
    own = jnp.dot(normed, own_ref[:width, :], preferred_element_type=jnp.float32)
    other = jnp.dot(normed, other_ref[:width, :], preferred_element_type=jnp.float32)
    keys = jnp.where(core == 0, own, other)
    values = jnp.where(core == 0, other, own)
    cosines, sines = cosines_ref[...], sines_ref[...]
    for head in range(KVH):
        part = keys[:, head * HD : (head + 1) * HD]
        out_ref[:, head * HD : (head + 1) * HD] = (
            part * cosines + pltpu.roll(part, HD // 2, 1) * sines
        ).astype(jnp.bfloat16)
    out_ref[:, KVH * HD :] = values.astype(jnp.bfloat16)


def exchange(value, axes, count, shift):
    return lax.ppermute(value, axes, [(i, i ^ shift) for i in range(count)])


def sum_on_cube(own, first, second, shard):
    width, half = own.shape
    f32, bf16 = jnp.float32, jnp.bfloat16
    shape = jax.ShapeDtypeStruct
    rows = shard // 2
    kept, *given = call(
        pair_kernel,
        (shape((4, rows, half), f32),) + (shape((4, rows, half), bf16),) * 3,
        (own, first, second),
    )
    pair_done = kept
    taken = [
        exchange(given[0], ("outer", "fsdp"), 16, 9),
        exchange(given[1], "fsdp", 8, 1),
        exchange(given[2], "outer", 2, 1),
    ]
    first_xy, second_xy, third_xy = taken
    kept, *given = call(
        z_kernel,
        (shape((rows, half), f32),) + (shape((rows, half), bf16),) * 3,
        (kept, *taken),
        flops=2 * 10**9,
    )
    taken = [exchange(given[i], "fsdp", 8, 2 * i + 2) for i in (1, 2, 0)]
    mine = call(last_kernel, shape((rows, half), bf16), (kept, *taken))
    return mine, (pair_done, pair_done, pair_done, mine)


def gather_on_cube(folded, steps):
    shard, half = folded.shape
    shape = jax.ShapeDtypeStruct

    def over(part, shift):
        return exchange(part, "fsdp", 8, shift)

    def stack(*parts, after):
        out = shape((len(parts), shard, half), folded.dtype)
        return call(stack_kernel, out, parts, after=after)

    near, far = over(folded, 2), over(folded, 4)
    both = over(stack(far, after=steps[0])[0], 2)
    low = stack(folded, near, after=steps[1])
    high = stack(far, both, after=steps[2])
    shifts = (0, 2, 4, 6, 1, 3, 5, 7)
    mine = steps[3]
    return call(
        functools.partial(bundle_kernel, shifts),
        shape((8 * shard + mine.shape[0], half), folded.dtype),
        (mine, low, high, over(low, 1), over(high, 1)),
    )


def body(outer, members, tokens, gain, kv_weight, positions, cotangent, counts, ratios):
    domains = 2 * outer
    rows, width = tokens.shape
    shard, columns = kv_weight.shape
    half = columns // 2
    f32, bf16 = jnp.float32, jnp.bfloat16
    shape = jax.ShapeDtypeStruct
    on_cube = outer == 2 and members == 8 and shard % 32 == 0

    exponents = np.arange(HD, dtype=np.float64) % (HD // 2) * (2.0 / HD)
    frequency = jnp.asarray(np.power(1000000.0, -exponents).astype(np.float32))
    normed, cosines, sines, both, given, folded = call(
        backward_kernel,
        (
            shape((rows, width), bf16),
            shape((rows, HD), f32),
            shape((rows, HD), f32),
            shape((rows, columns), bf16),
            shape((width - width // 4, half), bf16),
            shape((shard, half), bf16),
        ),
        (
            positions.reshape(rows // 128, 128),
            frequency.reshape(1, HD),
            counts,
            ratios.reshape(1, domains),
            cotangent,
            tokens,
            gain,
            kv_weight,
        ),
        fetched=8,
    )
    first = exchange(given, "core", 2, 1)
    own, given = call(
        rest_kernel, (shape((width, half), f32), shape((width // 4, half), bf16)), (normed, both)
    )
    second = exchange(given, "core", 2, 1)
    if on_cube:
        mine, steps = sum_on_cube(own, first, second, shard)
        own_half = gather_on_cube(folded, steps)
        other_half = exchange(own_half, "core", 2, 1)
        sums = [mine, other_half] + [exchange(mine, ("outer", "core"), 4, i) for i in (2, 3)]
    else:
        pair = own + jnp.concatenate([first, second]).astype(f32)
        pair = lax.psum_scatter(pair, "fsdp", scatter_dimension=0, tiled=True)
        mine = lax.psum(pair, "outer")
        own_half = lax.all_gather(folded, "fsdp", axis=0, tiled=True)
        other_half = exchange(own_half, "core", 2, 1)
        sums = [mine, exchange(mine, "core", 2, 1)]
    keys_out = call(
        forward_kernel,
        shape((rows, columns), bf16),
        (normed, own_half, other_half, cosines, sines),
        after=mine,
    )
    weight_grad, gain_grad = call(
        finish_kernel,
        (shape((shard, columns), f32), shape((shard,), f32)),
        (counts, gain, kv_weight, *sums),
        scratch=[pltpu.VMEM((shard, columns), f32)],
        after=keys_out,
        in_hbm=True,
    )
    return (keys_out, weight_grad, gain_grad)


def solution(mesh):
    domains, members = mesh.shape["dom"], mesh.shape["fsdp"]
    outer = domains // 2
    split = Mesh(mesh.devices.reshape(outer, 2, members), EVERY)
    return jax.shard_map(
        functools.partial(body, outer, members),
        mesh=split,
        in_specs=(
            P(EVERY, None),
            P("fsdp"),
            P("fsdp", None),
            P(EVERY),
            P(EVERY, None),
            P(),
            P(),
        ),
        out_specs=(P(EVERY, None), P("fsdp", None), P("fsdp")),
        check_vma=False,
    )
```

profile of v0, /device:TPU:0, one launch (start us, length us, event | category | flops | bytes accessed | tf_op | source)
XLA Modules:
  0.0 35.4 jit_solution(10563061814527066453)
XLA Ops:
  0.6 2.2 %shard_map.103 = (bf16[256,1536]{1,0:T(8,128)(2,1)S(1)}, f32[256,128]{1,0:T(8,128)S(1)}, f32[256,128]{1,0:T(8,128)S(1)}, bf16[256,512]{1,0:T(8,128)(2,1)S(1)}, b...) custom-call(s32[2,128]{1,0:T(2,128)} %bitcast.4, f32[1,128]{1,0:T(1,128)} %constant.3.frequency_hbm, ...), custom_call_target="tpu_custom_call" | custom-call | bytes 1000000 | tf_op jit(solution)/shard_map/pallas_call | solution.py:92
  2.8 0.5 %collective-permute-start = (bf16[1152,256]{1,0:T(8,128)(2,1)S(1)}, bf16[1152,256]{1,0:T(8,128)(2,1)S(1)}, u32[]{:S(2)}, u32[]{:S(2)}) collective-permute-start(bf16[1152,256]{1,0:T(8,128)(2,1)S(1)} %get-tuple-element.24), channel_id=1, source_target_pairs={{0,8},{8,0},{1,9},{9,1},{2,10},{10,2},{3,11},{11,3},{4,12},{12,4},... | collective-permute-start | bytes 1769480 | tf_op jit(solution)/shard_map/ppermute | solution.py:299
  3.4 0.5 %shard_map.104 = (f32[1536,256]{1,0:T(8,128)S(1)}, bf16[384,256]{1,0:T(8,128)(2,1)S(1)}) custom-call(bf16[256,1536]{1,0:T(8,128)(2,1)S(1)} %get-tuple-element.21.normed_ref.refs_0_, bf16[256,512]{1,0:T(8,128)(2,1)S(1)} %get-tuple-element.22.both_ref), custom_call_target="tpu_custom_call" | custom-call | bytes 1000000 | tf_op jit(solution)/shard_map/pallas_call | solution.py:92
  3.8 0.1 collective-permute-start.1
  4.0 4.0 %collective-permute-start.9 = (bf16[192,256]{1,0:T(8,128)(2,1)S(1)}, bf16[192,256]{1,0:T(8,128)(2,1)S(1)}, u32[]{:S(2)}, u32[]{:S(2)}) collective-permute-start(bf16[192,256]{1,0:T(8,128)(2,1)S(1)} %get-tuple-element.34.refs_0_), channel_id=1, source_target_pairs={{0,4},{1,5},{2,6},{3,7},{4,0},{5,1},{6,2},{7,3},{8,12},{9,13},{10,... | collective-permute-start | bytes 294920 | tf_op jit(solution)/shard_map/ppermute | solution.py:299
  8.0 0.1 shard_map.105
  8.1 2.5 %collective-permute-start.2 = (bf16[4,96,256]{2,1,0:T(8,128)(2,1)S(1)}, bf16[4,96,256]{2,1,0:T(8,128)(2,1)S(1)}, u32[]{:S(2)}, u32[]{:S(2)}) collective-permute-start(bf16[4,96,256]{2,1,0:T(8,128)(2,1)S(1)} %get-tuple-element.27), channel_id=1, source_target_pairs={{0,17},{1,16},{2,19},{3,18},{4,21},{5,20},{6,23},{7,22},{16,1},{17... | collective-permute-start | bytes 589832 | tf_op jit(solution)/shard_map/ppermute | solution.py:299
  10.6 0.5 %collective-permute-start.3 = (bf16[4,96,256]{2,1,0:T(8,128)(2,1)S(1)}, bf16[4,96,256]{2,1,0:T(8,128)(2,1)S(1)}, u32[]{:S(2)}, u32[]{:S(2)}) collective-permute-start(bf16[4,96,256]{2,1,0:T(8,128)(2,1)S(1)} %get-tuple-element.28), channel_id=1, source_target_pairs={{0,1},{1,0},{2,3},{3,2},{4,5},{5,4},{6,7},{7,6},{8,9},{9,8},{10,11... | collective-permute-start | bytes 589832 | tf_op jit(solution)/shard_map/ppermute | solution.py:299
  11.2 0.5 %collective-permute-start.4 = (bf16[4,96,256]{2,1,0:T(8,128)(2,1)S(1)}, bf16[4,96,256]{2,1,0:T(8,128)(2,1)S(1)}, u32[]{:S(2)}, u32[]{:S(2)}) collective-permute-start(bf16[4,96,256]{2,1,0:T(8,128)(2,1)S(1)} %get-tuple-element.29), channel_id=1, source_target_pairs={{0,16},{16,0},{1,17},{17,1},{2,18},{18,2},{3,19},{19,3},{4,20},{20... | collective-permute-start | bytes 589832 | tf_op jit(solution)/shard_map/ppermute | solution.py:299
  11.7 1.6 %collective-permute-start.8 = (bf16[192,256]{1,0:T(8,128)(2,1)S(1)}, bf16[192,256]{1,0:T(8,128)(2,1)S(1)}, u32[]{:S(2)}, u32[]{:S(2)}) collective-permute-start(bf16[192,256]{1,0:T(8,128)(2,1)S(1)} %get-tuple-element.34.refs_0_), channel_id=1, source_target_pairs={{0,2},{1,3},{2,0},{3,1},{4,6},{5,7},{6,4},{7,5},{8,10},{9,11},{10,... | collective-permute-start | bytes 294920 | tf_op jit(solution)/shard_map/ppermute | solution.py:299
  13.3 0.6 %collective-permute-start.10 = (bf16[192,256]{1,0:T(8,128)(2,1)S(1)}, bf16[192,256]{1,0:T(8,128)(2,1)S(1)}, u32[]{:S(2)}, u32[]{:S(2)}) collective-permute-start(bf16[192,256]{1,0:T(8,128)(2,1)S(1)} %bitcast.3), channel_id=1, source_target_pairs={{0,2},{1,3},{2,0},{3,1},{4,6},{5,7},{6,4},{7,5},{8,10},{9,11},{10,... | collective-permute-start | bytes 294920 | tf_op jit(solution)/shard_map/ppermute | solution.py:299
  13.9 3.4 %collective-permute-done.8.refs_1_ = bf16[192,256]{1,0:T(8,128)(2,1)S(1)} collective-permute-done((bf16[192,256]{1,0:T(8,128)(2,1)S(1)}, bf16[192,256]{1,0:T(8,128)(2,1)S(1)}, u32[]{:S(2)}, u32[]{:S(2)}) %collective-permute-start.8) | collective-permute-done | bytes 98336 | tf_op jit(solution)/shard_map/ppermute | solution.py:299
  17.3 1.5 %collective-permute-start.11 = (bf16[2,192,256]{2,1,0:T(8,128)(2,1)S(1)}, bf16[2,192,256]{2,1,0:T(8,128)(2,1)S(1)}, u32[]{:S(2)}, u32[]{:S(2)}) collective-permute-start(bf16[2,192,256]{2,1,0:T(8,128)(2,1)S(1)} %shard_map.108.refs_0_), channel_id=1, source_target_pairs={{0,1},{1,0},{2,3},{3,2},{4,5},{5,4},{6,7},{7,6},{8,9},{9,8},{10,11... | collective-permute-start | bytes 589832 | tf_op jit(solution)/shard_map/ppermute | solution.py:299
  18.8 1.0 %collective-permute-start.12 = (bf16[2,192,256]{2,1,0:T(8,128)(2,1)S(1)}, bf16[2,192,256]{2,1,0:T(8,128)(2,1)S(1)}, u32[]{:S(2)}, u32[]{:S(2)}) collective-permute-start(bf16[2,192,256]{2,1,0:T(8,128)(2,1)S(1)} %shard_map.110.refs_1_), channel_id=1, source_target_pairs={{0,1},{1,0},{2,3},{3,2},{4,5},{5,4},{6,7},{7,6},{8,9},{9,8},{10,11... | collective-permute-start | bytes 589832 | tf_op jit(solution)/shard_map/ppermute | solution.py:299
  19.8 1.4 %collective-permute-done.3.second_ref = bf16[4,96,256]{2,1,0:T(8,128)(2,1)S(1)} collective-permute-done((bf16[4,96,256]{2,1,0:T(8,128)(2,1)S(1)}, bf16[4,96,256]{2,1,0:T(8,128)(2,1)S(1)}, u32[]{:S(2)}, u32[]{:S(2)}) %collective-permute-start.3) | collective-permute-done | bytes 196640 | tf_op jit(solution)/shard_map/ppermute | solution.py:299
  21.2 0.1 shard_map.106
  21.3 1.2 %collective-permute-start.5 = (bf16[96,256]{1,0:T(8,128)(2,1)S(1)}, bf16[96,256]{1,0:T(8,128)(2,1)S(1)}, u32[]{:S(2)}, u32[]{:S(2)}) collective-permute-start(bf16[96,256]{1,0:T(8,128)(2,1)S(1)} %get-tuple-element.31), channel_id=1, source_target_pairs={{0,4},{1,5},{2,6},{3,7},{4,0},{5,1},{6,2},{7,3},{8,12},{9,13},{10,... | collective-permute-start | bytes 147464 | tf_op jit(solution)/shard_map/ppermute | solution.py:299
  22.5 2.8 %collective-permute-start.6 = (bf16[96,256]{1,0:T(8,128)(2,1)S(1)}, bf16[96,256]{1,0:T(8,128)(2,1)S(1)}, u32[]{:S(2)}, u32[]{:S(2)}) collective-permute-start(bf16[96,256]{1,0:T(8,128)(2,1)S(1)} %get-tuple-element.32), channel_id=1, source_target_pairs={{0,6},{1,7},{2,4},{3,5},{4,2},{5,3},{6,0},{7,1},{8,14},{9,15},{10,... | collective-permute-start | bytes 147464 | tf_op jit(solution)/shard_map/ppermute | solution.py:299
  25.3 1.7 %collective-permute-done.5.refs_0_ = bf16[96,256]{1,0:T(8,128)(2,1)S(1)} collective-permute-done((bf16[96,256]{1,0:T(8,128)(2,1)S(1)}, bf16[96,256]{1,0:T(8,128)(2,1)S(1)}, u32[]{:S(2)}, u32[]{:S(2)}) %collective-permute-start.5) | collective-permute-done | bytes 49184 | tf_op jit(solution)/shard_map/ppermute | solution.py:299
  27.0 1.5 %collective-permute-done.6.refs_1_ = bf16[96,256]{1,0:T(8,128)(2,1)S(1)} collective-permute-done((bf16[96,256]{1,0:T(8,128)(2,1)S(1)}, bf16[96,256]{1,0:T(8,128)(2,1)S(1)}, u32[]{:S(2)}, u32[]{:S(2)}) %collective-permute-start.6) | collective-permute-done | bytes 49184 | tf_op jit(solution)/shard_map/ppermute | solution.py:299
  28.5 0.9 %collective-permute-done.7.refs_2_ = bf16[96,256]{1,0:T(8,128)(2,1)S(1)} collective-permute-done((bf16[96,256]{1,0:T(8,128)(2,1)S(1)}, bf16[96,256]{1,0:T(8,128)(2,1)S(1)}, u32[]{:S(2)}, u32[]{:S(2)}) %collective-permute-start.7) | collective-permute-done | bytes 49184 | tf_op jit(solution)/shard_map/ppermute | solution.py:299
  29.4 0.1 shard_map.111.refs_1_
  29.5 0.0 copy-start
  29.5 0.0 copy-start.1
  29.6 0.1 collective-permute-start.13
  29.6 0.8 %collective-permute-start.14 = (bf16[96,256]{1,0:T(8,128)(2,1)S(1)}, bf16[96,256]{1,0:T(8,128)(2,1)S(1)}, u32[]{:S(2)}, u32[]{:S(2)}) collective-permute-start(bf16[96,256]{1,0:T(8,128)(2,1)S(1)} %shard_map.107.mine_ref.refs_5_.refs_3_), channel_id=1, source_target_pairs={{0,16},{8,24},{16,0},{24,8},{1,17},{9,25},{17,1},{25,9},{2,18},{10... | collective-permute-start | bytes 147464 | tf_op jit(solution)/shard_map/ppermute | solution.py:299
  30.4 1.1 %collective-permute-start.15 = (bf16[96,256]{1,0:T(8,128)(2,1)S(1)}, bf16[96,256]{1,0:T(8,128)(2,1)S(1)}, u32[]{:S(2)}, u32[]{:S(2)}) collective-permute-start(bf16[96,256]{1,0:T(8,128)(2,1)S(1)} %shard_map.107.mine_ref.refs_5_.refs_3_), channel_id=1, source_target_pairs={{0,24},{8,16},{16,8},{24,0},{1,25},{9,17},{17,9},{25,1},{2,26},{10... | collective-permute-start | bytes 147464 | tf_op jit(solution)/shard_map/ppermute | solution.py:299
  31.5 0.5 %collective-permute-done.13.refs_2_.refs_4_ = bf16[1632,256]{1,0:T(8,128)(2,1)S(1)} collective-permute-done((bf16[1632,256]{1,0:T(8,128)(2,1)S(1)}, bf16[1632,256]{1,0:T(8,128)(2,1)S(1)}, u32[]{:S(2)}, u32[]{:S(2)}) %collective-permute-start.13) | collective-permute-done | bytes 835616 | tf_op jit(solution)/shard_map/ppermute | solution.py:299
  32.0 1.3 %shard_map.112.refs_7_ = bf16[256,512]{1,0:T(8,128)(2,1)} custom-call(bf16[256,1536]{1,0:T(8,128)(2,1)S(1)} %get-tuple-element.21.normed_ref.refs_0_, bf16[1632,256]{1,0:T(8,128)(2,1)S(1)} %shard_map.111.refs_1_, bf16[1632,256]{1,0:T(8,128)(2,1)S(1)} %collective-permute-done.13.refs_2_.refs_4_, f32[256,128]{1,0:T(8,128)S(1)} %get-tuple-element.35.refs_3_, ...), custom_call_target="tpu_custom_call" | custom-call | bytes 1000000 | tf_op jit(solution)/shard_map/pallas_call | solution.py:92
  33.3 0.9 %collective-permute-done.14.refs_5_ = bf16[96,256]{1,0:T(8,128)(2,1)S(1)} collective-permute-done((bf16[96,256]{1,0:T(8,128)(2,1)S(1)}, bf16[96,256]{1,0:T(8,128)(2,1)S(1)}, u32[]{:S(2)}, u32[]{:S(2)}) %collective-permute-start.14) | collective-permute-done | bytes 49184 | tf_op jit(solution)/shard_map/ppermute | solution.py:299
  34.2 0.2 collective-permute-done.15.refs_6_
  34.5 0.9 %shard_map.113 = (f32[192,512]{1,0:T(8,128)}, f32[192]{0:T(256)}) custom-call(s32[4,8]{1,0:T(4,128)S(1)} %copy-done.1, bf16[192]{0:T(256)(128)(2,1)S(1)} %copy-done.2, bf16[192,512]{1,0:T(8,128)(2,1)S(1)} %copy-done, bf16[96,256]{1,0:T(8,128)(2,1)S(1)} %shard_map.107.mine_ref.refs_5_.refs_3_, bf16[1632,256]{1,0:T(8,128)(2,1)S(1)} %collective-permute-done.13.refs_2_.refs_4_, ...), custom_call_target="tpu_custom_call" | custom-call | bytes 1000000 | tf_op jit(solution)/shard_map/pallas_call | solution.py:92
  (17 shorter events, 0.1 us)
Async XLA Ops:
  2.8 5.2 %collective-permute-start = (bf16[1152,256]{1,0:T(8,128)(2,1)S(1)}, bf16[1152,256]{1,0:T(8,128)(2,1)S(1)}, u32[]{:S(2)}, u32[]{:S(2)}) collective-permute-start(bf16[1152,256]{1,0:T(8,128)(2,1)S(1)} %get-tuple-element.24), channel_id=1, source_target_pairs={{0,8},{8,0},{1,9},{9,1},{2,10},{10,2},{3,11},{11,3},{4,12},{12,4},... | collective-permute-start | bytes 1769480 | tf_op jit(solution)/shard_map/ppermute | solution.py:299
  3.8 4.2 %collective-permute-start.1 = (bf16[384,256]{1,0:T(8,128)(2,1)S(1)}, bf16[384,256]{1,0:T(8,128)(2,1)S(1)}, u32[]{:S(2)}, u32[]{:S(2)}) collective-permute-start(bf16[384,256]{1,0:T(8,128)(2,1)S(1)} %get-tuple-element.25), channel_id=1, source_target_pairs={{0,8},{8,0},{1,9},{9,1},{2,10},{10,2},{3,11},{11,3},{4,12},{12,4},... | collective-permute-start | bytes 589832 | tf_op jit(solution)/shard_map/ppermute | solution.py:299
  4.0 9.3 %collective-permute-start.9 = (bf16[192,256]{1,0:T(8,128)(2,1)S(1)}, bf16[192,256]{1,0:T(8,128)(2,1)S(1)}, u32[]{:S(2)}, u32[]{:S(2)}) collective-permute-start(bf16[192,256]{1,0:T(8,128)(2,1)S(1)} %get-tuple-element.34.refs_0_), channel_id=1, source_target_pairs={{0,4},{1,5},{2,6},{3,7},{4,0},{5,1},{6,2},{7,3},{8,12},{9,13},{10,... | collective-permute-start | bytes 294920 | tf_op jit(solution)/shard_map/ppermute | solution.py:299
  8.1 11.7 %collective-permute-start.2 = (bf16[4,96,256]{2,1,0:T(8,128)(2,1)S(1)}, bf16[4,96,256]{2,1,0:T(8,128)(2,1)S(1)}, u32[]{:S(2)}, u32[]{:S(2)}) collective-permute-start(bf16[4,96,256]{2,1,0:T(8,128)(2,1)S(1)} %get-tuple-element.27), channel_id=1, source_target_pairs={{0,17},{1,16},{2,19},{3,18},{4,21},{5,20},{6,23},{7,22},{16,1},{17... | collective-permute-start | bytes 589832 | tf_op jit(solution)/shard_map/ppermute | solution.py:299
  10.6 10.6 %collective-permute-start.3 = (bf16[4,96,256]{2,1,0:T(8,128)(2,1)S(1)}, bf16[4,96,256]{2,1,0:T(8,128)(2,1)S(1)}, u32[]{:S(2)}, u32[]{:S(2)}) collective-permute-start(bf16[4,96,256]{2,1,0:T(8,128)(2,1)S(1)} %get-tuple-element.28), channel_id=1, source_target_pairs={{0,1},{1,0},{2,3},{3,2},{4,5},{5,4},{6,7},{7,6},{8,9},{9,8},{10,11... | collective-permute-start | bytes 589832 | tf_op jit(solution)/shard_map/ppermute | solution.py:299
  11.2 10.0 %collective-permute-start.4 = (bf16[4,96,256]{2,1,0:T(8,128)(2,1)S(1)}, bf16[4,96,256]{2,1,0:T(8,128)(2,1)S(1)}, u32[]{:S(2)}, u32[]{:S(2)}) collective-permute-start(bf16[4,96,256]{2,1,0:T(8,128)(2,1)S(1)} %get-tuple-element.29), channel_id=1, source_target_pairs={{0,16},{16,0},{1,17},{17,1},{2,18},{18,2},{3,19},{19,3},{4,20},{20... | collective-permute-start | bytes 589832 | tf_op jit(solution)/shard_map/ppermute | solution.py:299
  11.7 5.6 %collective-permute-start.8 = (bf16[192,256]{1,0:T(8,128)(2,1)S(1)}, bf16[192,256]{1,0:T(8,128)(2,1)S(1)}, u32[]{:S(2)}, u32[]{:S(2)}) collective-permute-start(bf16[192,256]{1,0:T(8,128)(2,1)S(1)} %get-tuple-element.34.refs_0_), channel_id=1, source_target_pairs={{0,2},{1,3},{2,0},{3,1},{4,6},{5,7},{6,4},{7,5},{8,10},{9,11},{10,... | collective-permute-start | bytes 294920 | tf_op jit(solution)/shard_map/ppermute | solution.py:299
  13.3 5.5 %collective-permute-start.10 = (bf16[192,256]{1,0:T(8,128)(2,1)S(1)}, bf16[192,256]{1,0:T(8,128)(2,1)S(1)}, u32[]{:S(2)}, u32[]{:S(2)}) collective-permute-start(bf16[192,256]{1,0:T(8,128)(2,1)S(1)} %bitcast.3), channel_id=1, source_target_pairs={{0,2},{1,3},{2,0},{3,1},{4,6},{5,7},{6,4},{7,5},{8,10},{9,11},{10,... | collective-permute-start | bytes 294920 | tf_op jit(solution)/shard_map/ppermute | solution.py:299
  17.3 12.2 %collective-permute-start.11 = (bf16[2,192,256]{2,1,0:T(8,128)(2,1)S(1)}, bf16[2,192,256]{2,1,0:T(8,128)(2,1)S(1)}, u32[]{:S(2)}, u32[]{:S(2)}) collective-permute-start(bf16[2,192,256]{2,1,0:T(8,128)(2,1)S(1)} %shard_map.108.refs_0_), channel_id=1, source_target_pairs={{0,1},{1,0},{2,3},{3,2},{4,5},{5,4},{6,7},{7,6},{8,9},{9,8},{10,11... | collective-permute-start | bytes 589832 | tf_op jit(solution)/shard_map/ppermute | solution.py:299
  18.8 10.6 %collective-permute-start.12 = (bf16[2,192,256]{2,1,0:T(8,128)(2,1)S(1)}, bf16[2,192,256]{2,1,0:T(8,128)(2,1)S(1)}, u32[]{:S(2)}, u32[]{:S(2)}) collective-permute-start(bf16[2,192,256]{2,1,0:T(8,128)(2,1)S(1)} %shard_map.110.refs_1_), channel_id=1, source_target_pairs={{0,1},{1,0},{2,3},{3,2},{4,5},{5,4},{6,7},{7,6},{8,9},{9,8},{10,11... | collective-permute-start | bytes 589832 | tf_op jit(solution)/shard_map/ppermute | solution.py:299
  21.3 5.7 %collective-permute-start.5 = (bf16[96,256]{1,0:T(8,128)(2,1)S(1)}, bf16[96,256]{1,0:T(8,128)(2,1)S(1)}, u32[]{:S(2)}, u32[]{:S(2)}) collective-permute-start(bf16[96,256]{1,0:T(8,128)(2,1)S(1)} %get-tuple-element.31), channel_id=1, source_target_pairs={{0,4},{1,5},{2,6},{3,7},{4,0},{5,1},{6,2},{7,3},{8,12},{9,13},{10,... | collective-permute-start | bytes 147464 | tf_op jit(solution)/shard_map/ppermute | solution.py:299
  22.5 5.9 %collective-permute-start.6 = (bf16[96,256]{1,0:T(8,128)(2,1)S(1)}, bf16[96,256]{1,0:T(8,128)(2,1)S(1)}, u32[]{:S(2)}, u32[]{:S(2)}) collective-permute-start(bf16[96,256]{1,0:T(8,128)(2,1)S(1)} %get-tuple-element.32), channel_id=1, source_target_pairs={{0,6},{1,7},{2,4},{3,5},{4,2},{5,3},{6,0},{7,1},{8,14},{9,15},{10,... | collective-permute-start | bytes 147464 | tf_op jit(solution)/shard_map/ppermute | solution.py:299
  25.3 4.1 %collective-permute-start.7 = (bf16[96,256]{1,0:T(8,128)(2,1)S(1)}, bf16[96,256]{1,0:T(8,128)(2,1)S(1)}, u32[]{:S(2)}, u32[]{:S(2)}) collective-permute-start(bf16[96,256]{1,0:T(8,128)(2,1)S(1)} %get-tuple-element.33), channel_id=1, source_target_pairs={{0,2},{1,3},{2,0},{3,1},{4,6},{5,7},{6,4},{7,5},{8,10},{9,11},{10,... | collective-permute-start | bytes 147464 | tf_op jit(solution)/shard_map/ppermute | solution.py:299
  29.5 4.9 %copy-start = (bf16[192,512]{1,0:T(8,128)(2,1)S(1)}, bf16[192,512]{1,0:T(8,128)(2,1)}, u32[]{:S(2)}) copy-start(bf16[192,512]{1,0:T(8,128)(2,1)} %refs_2_.1) | copy-start | bytes 589828
  29.5 4.9 %copy-start.1 = (s32[4,8]{1,0:T(4,128)S(1)}, s32[4,8]{1,0:T(4,128)}, u32[]{:S(2)}) copy-start(s32[4,8]{1,0:T(4,128)} %refs_0_.1) | copy-start | bytes 388
  29.5 4.9 %copy-start.2 = (bf16[192]{0:T(256)(128)(2,1)S(1)}, bf16[192]{0:T(256)(128)(2,1)}, u32[]{:S(2)}) copy-start(bf16[192]{0:T(256)(128)(2,1)} %refs_1_.1) | copy-start | bytes 1156
  29.6 2.4 %collective-permute-start.13 = (bf16[1632,256]{1,0:T(8,128)(2,1)S(1)}, bf16[1632,256]{1,0:T(8,128)(2,1)S(1)}, u32[]{:S(2)}, u32[]{:S(2)}) collective-permute-start(bf16[1632,256]{1,0:T(8,128)(2,1)S(1)} %shard_map.111.refs_1_), channel_id=1, source_target_pairs={{0,8},{8,0},{1,9},{9,1},{2,10},{10,2},{3,11},{11,3},{4,12},{12,4},... | collective-permute-start | bytes 2506760 | tf_op jit(solution)/shard_map/ppermute | solution.py:299
  29.6 4.6 %collective-permute-start.14 = (bf16[96,256]{1,0:T(8,128)(2,1)S(1)}, bf16[96,256]{1,0:T(8,128)(2,1)S(1)}, u32[]{:S(2)}, u32[]{:S(2)}) collective-permute-start(bf16[96,256]{1,0:T(8,128)(2,1)S(1)} %shard_map.107.mine_ref.refs_5_.refs_3_), channel_id=1, source_target_pairs={{0,16},{8,24},{16,0},{24,8},{1,17},{9,25},{17,1},{25,9},{2,18},{10... | collective-permute-start | bytes 147464 | tf_op jit(solution)/shard_map/ppermute | solution.py:299
  30.4 4.0 %collective-permute-start.15 = (bf16[96,256]{1,0:T(8,128)(2,1)S(1)}, bf16[96,256]{1,0:T(8,128)(2,1)S(1)}, u32[]{:S(2)}, u32[]{:S(2)}) collective-permute-start(bf16[96,256]{1,0:T(8,128)(2,1)S(1)} %shard_map.107.mine_ref.refs_5_.refs_3_), channel_id=1, source_target_pairs={{0,24},{8,16},{16,8},{24,0},{1,25},{9,17},{17,9},{25,1},{2,26},{10... | collective-permute-start | bytes 147464 | tf_op jit(solution)/shard_map/ppermute | solution.py:299
where the time goes:
time: 35.5 us; the launch traced here: 35.4 us
  starting transfers between devices  18.9 us (53%)
  waiting for transfers between devices  10.4 us (29%)
  Pallas kernels  5.3 us (15%)
  between operations  0.75 us (2%)
    ppermute x16, starting transfers between devices, exchange(): return lax.ppermute(value, axes, [(i, i ^ shift) for i in range(count)])  18.9 us
    ppermute x16, waiting for transfers between devices, exchange(): return lax.ppermute(value, axes, [(i, i ^ shift) for i in range(count)])  10.4 us
    pallas_call x11, Pallas kernels, call(): pl.pallas_call(run, out_shape=out_shape, in_specs=[pl.BlockSpec(memory_sp...  5.3 us
  transfers between devices with their start and end apart: 16, of which 8 were waited for; matrix products, arithmetic and copies ran while one was open for 0% of the time, Pallas kernels for 6%

commit v1 on v0

--- a/solution.py
+++ b/solution.py
@@ -322,7 +322,7 @@
         (kept, *taken),
         flops=2 * 10**9,
     )
-    taken = [exchange(given[i], "fsdp", 8, 2 * i + 2) for i in (1, 2, 0)]
+    taken = [exchange(given[i], "fsdp", 8, 2 * i + 2) for i in (2, 1, 0)]
     mine = call(last_kernel, shape((rows, half), bf16), (kept, *taken))
     return mine, (pair_done, pair_done, pair_done, mine)
 

time: 35.5 us -> 35.3 us (level)
  waiting for transfers between devices: 10.4 us -> 9.75 us
  starting transfers between devices: 18.9 us -> 19.4 us
    ppermute x16, waiting for transfers between devices: 10.4 us -> 9.75 us  [exchange(): return lax.ppermute(value, axes, [(i, i ^ shift) for i in range(count)])]
    ppermute x16, starting transfers between devices: 18.9 us -> 19.4 us  [exchange(): return lax.ppermute(value, axes, [(i, i ^ shift) for i in range(count)])]
where the time goes in v1:
time: 35.3 us; the launch traced here: 35.2 us
  starting transfers between devices  19.4 us (55%)
  waiting for transfers between devices  9.75 us (28%)
  Pallas kernels  5.3 us (15%)
  between operations  0.75 us (2%)
    ppermute x16, starting transfers between devices, exchange(): return lax.ppermute(value, axes, [(i, i ^ shift) for i in range(count)])  19.4 us
    ppermute x16, waiting for transfers between devices, exchange(): return lax.ppermute(value, axes, [(i, i ^ shift) for i in range(count)])  9.75 us
    pallas_call x11, Pallas kernels, call(): pl.pallas_call(run, out_shape=out_shape, in_specs=[pl.BlockSpec(memory_sp...  5.3 us
  transfers between devices with their start and end apart: 16, of which 8 were waited for; matrix products, arithmetic and copies ran while one was open for 0% of the time, Pallas kernels for 6%

profile of v1, /device:TPU:0, one launch (start us, length us, event | category | flops | bytes accessed | tf_op | source)
XLA Modules:
  0.0 35.2 jit_solution(15545377058735726254)
XLA Ops:
  0.6 2.2 %shard_map.103 = (bf16[256,1536]{1,0:T(8,128)(2,1)S(1)}, f32[256,128]{1,0:T(8,128)S(1)}, f32[256,128]{1,0:T(8,128)S(1)}, bf16[256,512]{1,0:T(8,128)(2,1)S(1)}, b...) custom-call(s32[2,128]{1,0:T(2,128)} %bitcast.4, f32[1,128]{1,0:T(1,128)} %constant.3.frequency_hbm, ...), custom_call_target="tpu_custom_call" | custom-call | bytes 1000000 | tf_op jit(solution)/shard_map/pallas_call | solution.py:92
  2.8 0.5 %collective-permute-start = (bf16[1152,256]{1,0:T(8,128)(2,1)S(1)}, bf16[1152,256]{1,0:T(8,128)(2,1)S(1)}, u32[]{:S(2)}, u32[]{:S(2)}) collective-permute-start(bf16[1152,256]{1,0:T(8,128)(2,1)S(1)} %get-tuple-element.24), channel_id=1, source_target_pairs={{0,8},{8,0},{1,9},{9,1},{2,10},{10,2},{3,11},{11,3},{4,12},{12,4},... | collective-permute-start | bytes 1769480 | tf_op jit(solution)/shard_map/ppermute | solution.py:299
  3.4 0.5 %shard_map.104 = (f32[1536,256]{1,0:T(8,128)S(1)}, bf16[384,256]{1,0:T(8,128)(2,1)S(1)}) custom-call(bf16[256,1536]{1,0:T(8,128)(2,1)S(1)} %get-tuple-element.21.normed_ref.refs_0_, bf16[256,512]{1,0:T(8,128)(2,1)S(1)} %get-tuple-element.22.both_ref), custom_call_target="tpu_custom_call" | custom-call | bytes 1000000 | tf_op jit(solution)/shard_map/pallas_call | solution.py:92
  3.8 0.1 collective-permute-start.1
  4.0 4.0 %collective-permute-start.9 = (bf16[192,256]{1,0:T(8,128)(2,1)S(1)}, bf16[192,256]{1,0:T(8,128)(2,1)S(1)}, u32[]{:S(2)}, u32[]{:S(2)}) collective-permute-start(bf16[192,256]{1,0:T(8,128)(2,1)S(1)} %get-tuple-element.34.refs_0_), channel_id=1, source_target_pairs={{0,4},{1,5},{2,6},{3,7},{4,0},{5,1},{6,2},{7,3},{8,12},{9,13},{10,... | collective-permute-start | bytes 294920 | tf_op jit(solution)/shard_map/ppermute | solution.py:299
  8.0 0.1 shard_map.105
  8.1 2.5 %collective-permute-start.2 = (bf16[4,96,256]{2,1,0:T(8,128)(2,1)S(1)}, bf16[4,96,256]{2,1,0:T(8,128)(2,1)S(1)}, u32[]{:S(2)}, u32[]{:S(2)}) collective-permute-start(bf16[4,96,256]{2,1,0:T(8,128)(2,1)S(1)} %get-tuple-element.27), channel_id=1, source_target_pairs={{0,17},{1,16},{2,19},{3,18},{4,21},{5,20},{6,23},{7,22},{16,1},{17... | collective-permute-start | bytes 589832 | tf_op jit(solution)/shard_map/ppermute | solution.py:299
  10.6 0.5 %collective-permute-start.3 = (bf16[4,96,256]{2,1,0:T(8,128)(2,1)S(1)}, bf16[4,96,256]{2,1,0:T(8,128)(2,1)S(1)}, u32[]{:S(2)}, u32[]{:S(2)}) collective-permute-start(bf16[4,96,256]{2,1,0:T(8,128)(2,1)S(1)} %get-tuple-element.28), channel_id=1, source_target_pairs={{0,1},{1,0},{2,3},{3,2},{4,5},{5,4},{6,7},{7,6},{8,9},{9,8},{10,11... | collective-permute-start | bytes 589832 | tf_op jit(solution)/shard_map/ppermute | solution.py:299
  11.2 0.5 %collective-permute-start.4 = (bf16[4,96,256]{2,1,0:T(8,128)(2,1)S(1)}, bf16[4,96,256]{2,1,0:T(8,128)(2,1)S(1)}, u32[]{:S(2)}, u32[]{:S(2)}) collective-permute-start(bf16[4,96,256]{2,1,0:T(8,128)(2,1)S(1)} %get-tuple-element.29), channel_id=1, source_target_pairs={{0,16},{16,0},{1,17},{17,1},{2,18},{18,2},{3,19},{19,3},{4,20},{20... | collective-permute-start | bytes 589832 | tf_op jit(solution)/shard_map/ppermute | solution.py:299
  11.7 1.6 %collective-permute-start.8 = (bf16[192,256]{1,0:T(8,128)(2,1)S(1)}, bf16[192,256]{1,0:T(8,128)(2,1)S(1)}, u32[]{:S(2)}, u32[]{:S(2)}) collective-permute-start(bf16[192,256]{1,0:T(8,128)(2,1)S(1)} %get-tuple-element.34.refs_0_), channel_id=1, source_target_pairs={{0,2},{1,3},{2,0},{3,1},{4,6},{5,7},{6,4},{7,5},{8,10},{9,11},{10,... | collective-permute-start | bytes 294920 | tf_op jit(solution)/shard_map/ppermute | solution.py:299
  13.3 0.6 %collective-permute-start.10 = (bf16[192,256]{1,0:T(8,128)(2,1)S(1)}, bf16[192,256]{1,0:T(8,128)(2,1)S(1)}, u32[]{:S(2)}, u32[]{:S(2)}) collective-permute-start(bf16[192,256]{1,0:T(8,128)(2,1)S(1)} %bitcast.3), channel_id=1, source_target_pairs={{0,2},{1,3},{2,0},{3,1},{4,6},{5,7},{6,4},{7,5},{8,10},{9,11},{10,... | collective-permute-start | bytes 294920 | tf_op jit(solution)/shard_map/ppermute | solution.py:299
  13.9 3.4 %collective-permute-done.8.refs_1_ = bf16[192,256]{1,0:T(8,128)(2,1)S(1)} collective-permute-done((bf16[192,256]{1,0:T(8,128)(2,1)S(1)}, bf16[192,256]{1,0:T(8,128)(2,1)S(1)}, u32[]{:S(2)}, u32[]{:S(2)}) %collective-permute-start.8) | collective-permute-done | bytes 98336 | tf_op jit(solution)/shard_map/ppermute | solution.py:299
  17.3 1.5 %collective-permute-start.11 = (bf16[2,192,256]{2,1,0:T(8,128)(2,1)S(1)}, bf16[2,192,256]{2,1,0:T(8,128)(2,1)S(1)}, u32[]{:S(2)}, u32[]{:S(2)}) collective-permute-start(bf16[2,192,256]{2,1,0:T(8,128)(2,1)S(1)} %shard_map.108.refs_0_), channel_id=1, source_target_pairs={{0,1},{1,0},{2,3},{3,2},{4,5},{5,4},{6,7},{7,6},{8,9},{9,8},{10,11... | collective-permute-start | bytes 589832 | tf_op jit(solution)/shard_map/ppermute | solution.py:299
  18.8 1.0 %collective-permute-start.12 = (bf16[2,192,256]{2,1,0:T(8,128)(2,1)S(1)}, bf16[2,192,256]{2,1,0:T(8,128)(2,1)S(1)}, u32[]{:S(2)}, u32[]{:S(2)}) collective-permute-start(bf16[2,192,256]{2,1,0:T(8,128)(2,1)S(1)} %shard_map.110.refs_1_), channel_id=1, source_target_pairs={{0,1},{1,0},{2,3},{3,2},{4,5},{5,4},{6,7},{7,6},{8,9},{9,8},{10,11... | collective-permute-start | bytes 589832 | tf_op jit(solution)/shard_map/ppermute | solution.py:299
  19.8 1.4 %collective-permute-done.3.second_ref = bf16[4,96,256]{2,1,0:T(8,128)(2,1)S(1)} collective-permute-done((bf16[4,96,256]{2,1,0:T(8,128)(2,1)S(1)}, bf16[4,96,256]{2,1,0:T(8,128)(2,1)S(1)}, u32[]{:S(2)}, u32[]{:S(2)}) %collective-permute-start.3) | collective-permute-done | bytes 196640 | tf_op jit(solution)/shard_map/ppermute | solution.py:299
  21.2 0.1 shard_map.106
  21.3 2.2 %collective-permute-start.5 = (bf16[96,256]{1,0:T(8,128)(2,1)S(1)}, bf16[96,256]{1,0:T(8,128)(2,1)S(1)}, u32[]{:S(2)}, u32[]{:S(2)}) collective-permute-start(bf16[96,256]{1,0:T(8,128)(2,1)S(1)} %get-tuple-element.31), channel_id=1, source_target_pairs={{0,6},{1,7},{2,4},{3,5},{4,2},{5,3},{6,0},{7,1},{8,14},{9,15},{10,... | collective-permute-start | bytes 147464 | tf_op jit(solution)/shard_map/ppermute | solution.py:299
  23.5 0.9 %collective-permute-start.6 = (bf16[96,256]{1,0:T(8,128)(2,1)S(1)}, bf16[96,256]{1,0:T(8,128)(2,1)S(1)}, u32[]{:S(2)}, u32[]{:S(2)}) collective-permute-start(bf16[96,256]{1,0:T(8,128)(2,1)S(1)} %get-tuple-element.32), channel_id=1, source_target_pairs={{0,4},{1,5},{2,6},{3,7},{4,0},{5,1},{6,2},{7,3},{8,12},{9,13},{10,... | collective-permute-start | bytes 147464 | tf_op jit(solution)/shard_map/ppermute | solution.py:299
  24.4 1.3 %collective-permute-start.7 = (bf16[96,256]{1,0:T(8,128)(2,1)S(1)}, bf16[96,256]{1,0:T(8,128)(2,1)S(1)}, u32[]{:S(2)}, u32[]{:S(2)}) collective-permute-start(bf16[96,256]{1,0:T(8,128)(2,1)S(1)} %get-tuple-element.33), channel_id=1, source_target_pairs={{0,2},{1,3},{2,0},{3,1},{4,6},{5,7},{6,4},{7,5},{8,10},{9,11},{10,... | collective-permute-start | bytes 147464 | tf_op jit(solution)/shard_map/ppermute | solution.py:299
  25.8 1.7 %collective-permute-done.5.refs_0_ = bf16[96,256]{1,0:T(8,128)(2,1)S(1)} collective-permute-done((bf16[96,256]{1,0:T(8,128)(2,1)S(1)}, bf16[96,256]{1,0:T(8,128)(2,1)S(1)}, u32[]{:S(2)}, u32[]{:S(2)}) %collective-permute-start.5) | collective-permute-done | bytes 49184 | tf_op jit(solution)/shard_map/ppermute | solution.py:299
  27.5 1.4 %collective-permute-done.6.refs_1_ = bf16[96,256]{1,0:T(8,128)(2,1)S(1)} collective-permute-done((bf16[96,256]{1,0:T(8,128)(2,1)S(1)}, bf16[96,256]{1,0:T(8,128)(2,1)S(1)}, u32[]{:S(2)}, u32[]{:S(2)}) %collective-permute-start.6) | collective-permute-done | bytes 49184 | tf_op jit(solution)/shard_map/ppermute | solution.py:299
  28.9 0.1 collective-permute-done.7.refs_2_
  29.1 0.1 shard_map.111.refs_1_
  29.2 0.0 copy-start.1
  29.2 0.1 collective-permute-start.13
  29.3 0.9 %collective-permute-start.14 = (bf16[96,256]{1,0:T(8,128)(2,1)S(1)}, bf16[96,256]{1,0:T(8,128)(2,1)S(1)}, u32[]{:S(2)}, u32[]{:S(2)}) collective-permute-start(bf16[96,256]{1,0:T(8,128)(2,1)S(1)} %shard_map.107.mine_ref.refs_5_.refs_3_), channel_id=1, source_target_pairs={{0,16},{8,24},{16,0},{24,8},{1,17},{9,25},{17,1},{25,9},{2,18},{10... | collective-permute-start | bytes 147464 | tf_op jit(solution)/shard_map/ppermute | solution.py:299
  30.2 1.0 %collective-permute-start.15 = (bf16[96,256]{1,0:T(8,128)(2,1)S(1)}, bf16[96,256]{1,0:T(8,128)(2,1)S(1)}, u32[]{:S(2)}, u32[]{:S(2)}) collective-permute-start(bf16[96,256]{1,0:T(8,128)(2,1)S(1)} %shard_map.107.mine_ref.refs_5_.refs_3_), channel_id=1, source_target_pairs={{0,24},{8,16},{16,8},{24,0},{1,25},{9,17},{17,9},{25,1},{2,26},{10... | collective-permute-start | bytes 147464 | tf_op jit(solution)/shard_map/ppermute | solution.py:299
  31.1 0.5 %collective-permute-done.13.refs_2_.refs_4_ = bf16[1632,256]{1,0:T(8,128)(2,1)S(1)} collective-permute-done((bf16[1632,256]{1,0:T(8,128)(2,1)S(1)}, bf16[1632,256]{1,0:T(8,128)(2,1)S(1)}, u32[]{:S(2)}, u32[]{:S(2)}) %collective-permute-start.13) | collective-permute-done | bytes 835616 | tf_op jit(solution)/shard_map/ppermute | solution.py:299
  31.6 1.3 %shard_map.112.refs_7_ = bf16[256,512]{1,0:T(8,128)(2,1)} custom-call(bf16[256,1536]{1,0:T(8,128)(2,1)S(1)} %get-tuple-element.21.normed_ref.refs_0_, bf16[1632,256]{1,0:T(8,128)(2,1)S(1)} %shard_map.111.refs_1_, bf16[1632,256]{1,0:T(8,128)(2,1)S(1)} %collective-permute-done.13.refs_2_.refs_4_, f32[256,128]{1,0:T(8,128)S(1)} %get-tuple-element.35.refs_3_, ...), custom_call_target="tpu_custom_call" | custom-call | bytes 1000000 | tf_op jit(solution)/shard_map/pallas_call | solution.py:92
  33.0 0.7 %collective-permute-done.14.refs_5_ = bf16[96,256]{1,0:T(8,128)(2,1)S(1)} collective-permute-done((bf16[96,256]{1,0:T(8,128)(2,1)S(1)}, bf16[96,256]{1,0:T(8,128)(2,1)S(1)}, u32[]{:S(2)}, u32[]{:S(2)}) %collective-permute-start.14) | collective-permute-done | bytes 49184 | tf_op jit(solution)/shard_map/ppermute | solution.py:299
  33.7 0.5 %collective-permute-done.15.refs_6_ = bf16[96,256]{1,0:T(8,128)(2,1)S(1)} collective-permute-done((bf16[96,256]{1,0:T(8,128)(2,1)S(1)}, bf16[96,256]{1,0:T(8,128)(2,1)S(1)}, u32[]{:S(2)}, u32[]{:S(2)}) %collective-permute-start.15) | collective-permute-done | bytes 49184 | tf_op jit(solution)/shard_map/ppermute | solution.py:299
  34.2 0.9 %shard_map.113 = (f32[192,512]{1,0:T(8,128)}, f32[192]{0:T(256)}) custom-call(s32[4,8]{1,0:T(4,128)S(1)} %copy-done.1, bf16[192]{0:T(256)(128)(2,1)S(1)} %copy-done.2, bf16[192,512]{1,0:T(8,128)(2,1)S(1)} %copy-done, bf16[96,256]{1,0:T(8,128)(2,1)S(1)} %shard_map.107.mine_ref.refs_5_.refs_3_, bf16[1632,256]{1,0:T(8,128)(2,1)S(1)} %collective-permute-done.13.refs_2_.refs_4_, ...), custom_call_target="tpu_custom_call" | custom-call | bytes 1000000 | tf_op jit(solution)/shard_map/pallas_call | solution.py:92
  (17 shorter events, 0.1 us)
Async XLA Ops:
  2.8 5.2 %collective-permute-start = (bf16[1152,256]{1,0:T(8,128)(2,1)S(1)}, bf16[1152,256]{1,0:T(8,128)(2,1)S(1)}, u32[]{:S(2)}, u32[]{:S(2)}) collective-permute-start(bf16[1152,256]{1,0:T(8,128)(2,1)S(1)} %get-tuple-element.24), channel_id=1, source_target_pairs={{0,8},{8,0},{1,9},{9,1},{2,10},{10,2},{3,11},{11,3},{4,12},{12,4},... | collective-permute-start | bytes 1769480 | tf_op jit(solution)/shard_map/ppermute | solution.py:299
  3.8 4.2 %collective-permute-start.1 = (bf16[384,256]{1,0:T(8,128)(2,1)S(1)}, bf16[384,256]{1,0:T(8,128)(2,1)S(1)}, u32[]{:S(2)}, u32[]{:S(2)}) collective-permute-start(bf16[384,256]{1,0:T(8,128)(2,1)S(1)} %get-tuple-element.25), channel_id=1, source_target_pairs={{0,8},{8,0},{1,9},{9,1},{2,10},{10,2},{3,11},{11,3},{4,12},{12,4},... | collective-permute-start | bytes 589832 | tf_op jit(solution)/shard_map/ppermute | solution.py:299
  4.0 9.3 %collective-permute-start.9 = (bf16[192,256]{1,0:T(8,128)(2,1)S(1)}, bf16[192,256]{1,0:T(8,128)(2,1)S(1)}, u32[]{:S(2)}, u32[]{:S(2)}) collective-permute-start(bf16[192,256]{1,0:T(8,128)(2,1)S(1)} %get-tuple-element.34.refs_0_), channel_id=1, source_target_pairs={{0,4},{1,5},{2,6},{3,7},{4,0},{5,1},{6,2},{7,3},{8,12},{9,13},{10,... | collective-permute-start | bytes 294920 | tf_op jit(solution)/shard_map/ppermute | solution.py:299
  8.1 11.7 %collective-permute-start.2 = (bf16[4,96,256]{2,1,0:T(8,128)(2,1)S(1)}, bf16[4,96,256]{2,1,0:T(8,128)(2,1)S(1)}, u32[]{:S(2)}, u32[]{:S(2)}) collective-permute-start(bf16[4,96,256]{2,1,0:T(8,128)(2,1)S(1)} %get-tuple-element.27), channel_id=1, source_target_pairs={{0,17},{1,16},{2,19},{3,18},{4,21},{5,20},{6,23},{7,22},{16,1},{17... | collective-permute-start | bytes 589832 | tf_op jit(solution)/shard_map/ppermute | solution.py:299
  10.6 10.6 %collective-permute-start.3 = (bf16[4,96,256]{2,1,0:T(8,128)(2,1)S(1)}, bf16[4,96,256]{2,1,0:T(8,128)(2,1)S(1)}, u32[]{:S(2)}, u32[]{:S(2)}) collective-permute-start(bf16[4,96,256]{2,1,0:T(8,128)(2,1)S(1)} %get-tuple-element.28), channel_id=1, source_target_pairs={{0,1},{1,0},{2,3},{3,2},{4,5},{5,4},{6,7},{7,6},{8,9},{9,8},{10,11... | collective-permute-start | bytes 589832 | tf_op jit(solution)/shard_map/ppermute | solution.py:299
  11.2 10.0 %collective-permute-start.4 = (bf16[4,96,256]{2,1,0:T(8,128)(2,1)S(1)}, bf16[4,96,256]{2,1,0:T(8,128)(2,1)S(1)}, u32[]{:S(2)}, u32[]{:S(2)}) collective-permute-start(bf16[4,96,256]{2,1,0:T(8,128)(2,1)S(1)} %get-tuple-element.29), channel_id=1, source_target_pairs={{0,16},{16,0},{1,17},{17,1},{2,18},{18,2},{3,19},{19,3},{4,20},{20... | collective-permute-start | bytes 589832 | tf_op jit(solution)/shard_map/ppermute | solution.py:299
  11.7 5.6 %collective-permute-start.8 = (bf16[192,256]{1,0:T(8,128)(2,1)S(1)}, bf16[192,256]{1,0:T(8,128)(2,1)S(1)}, u32[]{:S(2)}, u32[]{:S(2)}) collective-permute-start(bf16[192,256]{1,0:T(8,128)(2,1)S(1)} %get-tuple-element.34.refs_0_), channel_id=1, source_target_pairs={{0,2},{1,3},{2,0},{3,1},{4,6},{5,7},{6,4},{7,5},{8,10},{9,11},{10,... | collective-permute-start | bytes 294920 | tf_op jit(solution)/shard_map/ppermute | solution.py:299
  13.3 5.5 %collective-permute-start.10 = (bf16[192,256]{1,0:T(8,128)(2,1)S(1)}, bf16[192,256]{1,0:T(8,128)(2,1)S(1)}, u32[]{:S(2)}, u32[]{:S(2)}) collective-permute-start(bf16[192,256]{1,0:T(8,128)(2,1)S(1)} %bitcast.3), channel_id=1, source_target_pairs={{0,2},{1,3},{2,0},{3,1},{4,6},{5,7},{6,4},{7,5},{8,10},{9,11},{10,... | collective-permute-start | bytes 294920 | tf_op jit(solution)/shard_map/ppermute | solution.py:299
  17.3 11.8 %collective-permute-start.11 = (bf16[2,192,256]{2,1,0:T(8,128)(2,1)S(1)}, bf16[2,192,256]{2,1,0:T(8,128)(2,1)S(1)}, u32[]{:S(2)}, u32[]{:S(2)}) collective-permute-start(bf16[2,192,256]{2,1,0:T(8,128)(2,1)S(1)} %shard_map.108.refs_0_), channel_id=1, source_target_pairs={{0,1},{1,0},{2,3},{3,2},{4,5},{5,4},{6,7},{7,6},{8,9},{9,8},{10,11... | collective-permute-start | bytes 589832 | tf_op jit(solution)/shard_map/ppermute | solution.py:299
  18.8 10.3 %collective-permute-start.12 = (bf16[2,192,256]{2,1,0:T(8,128)(2,1)S(1)}, bf16[2,192,256]{2,1,0:T(8,128)(2,1)S(1)}, u32[]{:S(2)}, u32[]{:S(2)}) collective-permute-start(bf16[2,192,256]{2,1,0:T(8,128)(2,1)S(1)} %shard_map.110.refs_1_), channel_id=1, source_target_pairs={{0,1},{1,0},{2,3},{3,2},{4,5},{5,4},{6,7},{7,6},{8,9},{9,8},{10,11... | collective-permute-start | bytes 589832 | tf_op jit(solution)/shard_map/ppermute | solution.py:299
  21.3 6.2 %collective-permute-start.5 = (bf16[96,256]{1,0:T(8,128)(2,1)S(1)}, bf16[96,256]{1,0:T(8,128)(2,1)S(1)}, u32[]{:S(2)}, u32[]{:S(2)}) collective-permute-start(bf16[96,256]{1,0:T(8,128)(2,1)S(1)} %get-tuple-element.31), channel_id=1, source_target_pairs={{0,6},{1,7},{2,4},{3,5},{4,2},{5,3},{6,0},{7,1},{8,14},{9,15},{10,... | collective-permute-start | bytes 147464 | tf_op jit(solution)/shard_map/ppermute | solution.py:299
  23.5 5.3 %collective-permute-start.6 = (bf16[96,256]{1,0:T(8,128)(2,1)S(1)}, bf16[96,256]{1,0:T(8,128)(2,1)S(1)}, u32[]{:S(2)}, u32[]{:S(2)}) collective-permute-start(bf16[96,256]{1,0:T(8,128)(2,1)S(1)} %get-tuple-element.32), channel_id=1, source_target_pairs={{0,4},{1,5},{2,6},{3,7},{4,0},{5,1},{6,2},{7,3},{8,12},{9,13},{10,... | collective-permute-start | bytes 147464 | tf_op jit(solution)/shard_map/ppermute | solution.py:299
  24.4 4.6 %collective-permute-start.7 = (bf16[96,256]{1,0:T(8,128)(2,1)S(1)}, bf16[96,256]{1,0:T(8,128)(2,1)S(1)}, u32[]{:S(2)}, u32[]{:S(2)}) collective-permute-start(bf16[96,256]{1,0:T(8,128)(2,1)S(1)} %get-tuple-element.33), channel_id=1, source_target_pairs={{0,2},{1,3},{2,0},{3,1},{4,6},{5,7},{6,4},{7,5},{8,10},{9,11},{10,... | collective-permute-start | bytes 147464 | tf_op jit(solution)/shard_map/ppermute | solution.py:299
  29.2 5.1 %copy-start = (bf16[192,512]{1,0:T(8,128)(2,1)S(1)}, bf16[192,512]{1,0:T(8,128)(2,1)}, u32[]{:S(2)}) copy-start(bf16[192,512]{1,0:T(8,128)(2,1)} %refs_2_.1) | copy-start | bytes 589828
  29.2 5.1 %copy-start.1 = (s32[4,8]{1,0:T(4,128)S(1)}, s32[4,8]{1,0:T(4,128)}, u32[]{:S(2)}) copy-start(s32[4,8]{1,0:T(4,128)} %refs_0_.1) | copy-start | bytes 388
  29.2 5.0 %copy-start.2 = (bf16[192]{0:T(256)(128)(2,1)S(1)}, bf16[192]{0:T(256)(128)(2,1)}, u32[]{:S(2)}) copy-start(bf16[192]{0:T(256)(128)(2,1)} %refs_1_.1) | copy-start | bytes 1156
  29.2 2.4 %collective-permute-start.13 = (bf16[1632,256]{1,0:T(8,128)(2,1)S(1)}, bf16[1632,256]{1,0:T(8,128)(2,1)S(1)}, u32[]{:S(2)}, u32[]{:S(2)}) collective-permute-start(bf16[1632,256]{1,0:T(8,128)(2,1)S(1)} %shard_map.111.refs_1_), channel_id=1, source_target_pairs={{0,8},{8,0},{1,9},{9,1},{2,10},{10,2},{3,11},{11,3},{4,12},{12,4},... | collective-permute-start | bytes 2506760 | tf_op jit(solution)/shard_map/ppermute | solution.py:299
  29.3 4.4 %collective-permute-start.14 = (bf16[96,256]{1,0:T(8,128)(2,1)S(1)}, bf16[96,256]{1,0:T(8,128)(2,1)S(1)}, u32[]{:S(2)}, u32[]{:S(2)}) collective-permute-start(bf16[96,256]{1,0:T(8,128)(2,1)S(1)} %shard_map.107.mine_ref.refs_5_.refs_3_), channel_id=1, source_target_pairs={{0,16},{8,24},{16,0},{24,8},{1,17},{9,25},{17,1},{25,9},{2,18},{10... | collective-permute-start | bytes 147464 | tf_op jit(solution)/shard_map/ppermute | solution.py:299
  30.2 4.0 %collective-permute-start.15 = (bf16[96,256]{1,0:T(8,128)(2,1)S(1)}, bf16[96,256]{1,0:T(8,128)(2,1)S(1)}, u32[]{:S(2)}, u32[]{:S(2)}) collective-permute-start(bf16[96,256]{1,0:T(8,128)(2,1)S(1)} %shard_map.107.mine_ref.refs_5_.refs_3_), channel_id=1, source_target_pairs={{0,24},{8,16},{16,8},{24,0},{1,25},{9,17},{17,9},{25,1},{2,26},{10... | collective-permute-start | bytes 147464 | tf_op jit(solution)/shard_map/ppermute | solution.py:299

commit v2 on v1

--- a/solution.py
+++ b/solution.py
@@ -266,7 +266,7 @@
     live_total = full_sum(counts_ref[...].astype(jnp.float32)) * float(BLOCK)
     scale = 1.0 / jnp.sqrt(live_total)
     gains = to_column(gain_ref[...].astype(jnp.float32).reshape(1, -1)) * scale
-    shifts = (0, 1) if len(parts) == 2 else (0, 1, 2, 3)
+    shifts = (0, 1) if len(parts) == 2 else (0, 1, 3, 2)
     for shift, part_ref in zip(shifts, parts):
         at_y = 0 if len(parts) == 2 else jnp.bitwise_xor(y, shift // 2)
         at = jnp.bitwise_xor(core, shift % 2)
@@ -393,7 +393,7 @@
         mine, steps = sum_on_cube(own, first, second, shard)
         own_half = gather_on_cube(folded, steps)
         other_half = exchange(own_half, "core", 2, 1)
-        sums = [mine, other_half] + [exchange(mine, ("outer", "core"), 4, i) for i in (2, 3)]
+        sums = [mine, other_half] + [exchange(mine, ("outer", "core"), 4, i) for i in (3, 2)]
     else:
         pair = own + jnp.concatenate([first, second]).astype(f32)
         pair = lax.psum_scatter(pair, "fsdp", scatter_dimension=0, tiled=True)

time: 35.3 us -> 35.6 us (level)
  transfers between devices with their start and end apart: 16 -> 16, of which waited for: 8 -> 7; matrix products, arithmetic and copies ran while one was open for 0% -> 0% of each run, Pallas kernels for 6% -> 6%
where the time goes in v2:
time: 35.6 us; the launch traced here: 35.4 us
  starting transfers between devices  19.6 us (55%)
  waiting for transfers between devices  9.72 us (27%)
  Pallas kernels  5.3 us (15%)
  between operations  0.75 us (2%)
    ppermute x16, starting transfers between devices, exchange(): return lax.ppermute(value, axes, [(i, i ^ shift) for i in range(count)])  19.6 us
    ppermute x16, waiting for transfers between devices, exchange(): return lax.ppermute(value, axes, [(i, i ^ shift) for i in range(count)])  9.72 us
    pallas_call x11, Pallas kernels, call(): pl.pallas_call(run, out_shape=out_shape, in_specs=[pl.BlockSpec(memory_sp...  5.3 us
  transfers between devices with their start and end apart: 16, of which 7 were waited for; matrix products, arithmetic and copies ran while one was open for 0% of the time, Pallas kernels for 6%

profile of v2, /device:TPU:0, one launch (start us, length us, event | category | flops | bytes accessed | tf_op | source)
XLA Modules:
  0.0 35.4 jit_solution(2846265633613168311)
XLA Ops:
  0.6 2.2 %shard_map.103 = (bf16[256,1536]{1,0:T(8,128)(2,1)S(1)}, f32[256,128]{1,0:T(8,128)S(1)}, f32[256,128]{1,0:T(8,128)S(1)}, bf16[256,512]{1,0:T(8,128)(2,1)S(1)}, b...) custom-call(s32[2,128]{1,0:T(2,128)} %bitcast.4, f32[1,128]{1,0:T(1,128)} %constant.3.frequency_hbm, ...), custom_call_target="tpu_custom_call" | custom-call | bytes 1000000 | tf_op jit(solution)/shard_map/pallas_call | solution.py:92
  2.8 0.5 %collective-permute-start = (bf16[1152,256]{1,0:T(8,128)(2,1)S(1)}, bf16[1152,256]{1,0:T(8,128)(2,1)S(1)}, u32[]{:S(2)}, u32[]{:S(2)}) collective-permute-start(bf16[1152,256]{1,0:T(8,128)(2,1)S(1)} %get-tuple-element.24), channel_id=1, source_target_pairs={{0,8},{8,0},{1,9},{9,1},{2,10},{10,2},{3,11},{11,3},{4,12},{12,4},... | collective-permute-start | bytes 1769480 | tf_op jit(solution)/shard_map/ppermute | solution.py:299
  3.4 0.5 %shard_map.104 = (f32[1536,256]{1,0:T(8,128)S(1)}, bf16[384,256]{1,0:T(8,128)(2,1)S(1)}) custom-call(bf16[256,1536]{1,0:T(8,128)(2,1)S(1)} %get-tuple-element.21.normed_ref.refs_0_, bf16[256,512]{1,0:T(8,128)(2,1)S(1)} %get-tuple-element.22.both_ref), custom_call_target="tpu_custom_call" | custom-call | bytes 1000000 | tf_op jit(solution)/shard_map/pallas_call | solution.py:92
  3.8 0.1 collective-permute-start.1
  4.0 4.0 %collective-permute-start.9 = (bf16[192,256]{1,0:T(8,128)(2,1)S(1)}, bf16[192,256]{1,0:T(8,128)(2,1)S(1)}, u32[]{:S(2)}, u32[]{:S(2)}) collective-permute-start(bf16[192,256]{1,0:T(8,128)(2,1)S(1)} %get-tuple-element.34.refs_0_), channel_id=1, source_target_pairs={{0,4},{1,5},{2,6},{3,7},{4,0},{5,1},{6,2},{7,3},{8,12},{9,13},{10,... | collective-permute-start | bytes 294920 | tf_op jit(solution)/shard_map/ppermute | solution.py:299
  8.0 0.1 shard_map.105
  8.1 2.5 %collective-permute-start.2 = (bf16[4,96,256]{2,1,0:T(8,128)(2,1)S(1)}, bf16[4,96,256]{2,1,0:T(8,128)(2,1)S(1)}, u32[]{:S(2)}, u32[]{:S(2)}) collective-permute-start(bf16[4,96,256]{2,1,0:T(8,128)(2,1)S(1)} %get-tuple-element.27), channel_id=1, source_target_pairs={{0,17},{1,16},{2,19},{3,18},{4,21},{5,20},{6,23},{7,22},{16,1},{17... | collective-permute-start | bytes 589832 | tf_op jit(solution)/shard_map/ppermute | solution.py:299
  10.6 0.5 %collective-permute-start.3 = (bf16[4,96,256]{2,1,0:T(8,128)(2,1)S(1)}, bf16[4,96,256]{2,1,0:T(8,128)(2,1)S(1)}, u32[]{:S(2)}, u32[]{:S(2)}) collective-permute-start(bf16[4,96,256]{2,1,0:T(8,128)(2,1)S(1)} %get-tuple-element.28), channel_id=1, source_target_pairs={{0,1},{1,0},{2,3},{3,2},{4,5},{5,4},{6,7},{7,6},{8,9},{9,8},{10,11... | collective-permute-start | bytes 589832 | tf_op jit(solution)/shard_map/ppermute | solution.py:299
  11.2 0.5 %collective-permute-start.4 = (bf16[4,96,256]{2,1,0:T(8,128)(2,1)S(1)}, bf16[4,96,256]{2,1,0:T(8,128)(2,1)S(1)}, u32[]{:S(2)}, u32[]{:S(2)}) collective-permute-start(bf16[4,96,256]{2,1,0:T(8,128)(2,1)S(1)} %get-tuple-element.29), channel_id=1, source_target_pairs={{0,16},{16,0},{1,17},{17,1},{2,18},{18,2},{3,19},{19,3},{4,20},{20... | collective-permute-start | bytes 589832 | tf_op jit(solution)/shard_map/ppermute | solution.py:299
  11.7 1.6 %collective-permute-start.8 = (bf16[192,256]{1,0:T(8,128)(2,1)S(1)}, bf16[192,256]{1,0:T(8,128)(2,1)S(1)}, u32[]{:S(2)}, u32[]{:S(2)}) collective-permute-start(bf16[192,256]{1,0:T(8,128)(2,1)S(1)} %get-tuple-element.34.refs_0_), channel_id=1, source_target_pairs={{0,2},{1,3},{2,0},{3,1},{4,6},{5,7},{6,4},{7,5},{8,10},{9,11},{10,... | collective-permute-start | bytes 294920 | tf_op jit(solution)/shard_map/ppermute | solution.py:299
  13.3 0.6 %collective-permute-start.10 = (bf16[192,256]{1,0:T(8,128)(2,1)S(1)}, bf16[192,256]{1,0:T(8,128)(2,1)S(1)}, u32[]{:S(2)}, u32[]{:S(2)}) collective-permute-start(bf16[192,256]{1,0:T(8,128)(2,1)S(1)} %bitcast.3), channel_id=1, source_target_pairs={{0,2},{1,3},{2,0},{3,1},{4,6},{5,7},{6,4},{7,5},{8,10},{9,11},{10,... | collective-permute-start | bytes 294920 | tf_op jit(solution)/shard_map/ppermute | solution.py:299
  13.9 3.4 %collective-permute-done.8.refs_1_ = bf16[192,256]{1,0:T(8,128)(2,1)S(1)} collective-permute-done((bf16[192,256]{1,0:T(8,128)(2,1)S(1)}, bf16[192,256]{1,0:T(8,128)(2,1)S(1)}, u32[]{:S(2)}, u32[]{:S(2)}) %collective-permute-start.8) | collective-permute-done | bytes 98336 | tf_op jit(solution)/shard_map/ppermute | solution.py:299
  17.3 1.5 %collective-permute-start.11 = (bf16[2,192,256]{2,1,0:T(8,128)(2,1)S(1)}, bf16[2,192,256]{2,1,0:T(8,128)(2,1)S(1)}, u32[]{:S(2)}, u32[]{:S(2)}) collective-permute-start(bf16[2,192,256]{2,1,0:T(8,128)(2,1)S(1)} %shard_map.108.refs_0_), channel_id=1, source_target_pairs={{0,1},{1,0},{2,3},{3,2},{4,5},{5,4},{6,7},{7,6},{8,9},{9,8},{10,11... | collective-permute-start | bytes 589832 | tf_op jit(solution)/shard_map/ppermute | solution.py:299
  18.8 1.0 %collective-permute-start.12 = (bf16[2,192,256]{2,1,0:T(8,128)(2,1)S(1)}, bf16[2,192,256]{2,1,0:T(8,128)(2,1)S(1)}, u32[]{:S(2)}, u32[]{:S(2)}) collective-permute-start(bf16[2,192,256]{2,1,0:T(8,128)(2,1)S(1)} %shard_map.110.refs_1_), channel_id=1, source_target_pairs={{0,1},{1,0},{2,3},{3,2},{4,5},{5,4},{6,7},{7,6},{8,9},{9,8},{10,11... | collective-permute-start | bytes 589832 | tf_op jit(solution)/shard_map/ppermute | solution.py:299
  19.8 1.4 %collective-permute-done.3.second_ref = bf16[4,96,256]{2,1,0:T(8,128)(2,1)S(1)} collective-permute-done((bf16[4,96,256]{2,1,0:T(8,128)(2,1)S(1)}, bf16[4,96,256]{2,1,0:T(8,128)(2,1)S(1)}, u32[]{:S(2)}, u32[]{:S(2)}) %collective-permute-start.3) | collective-permute-done | bytes 196640 | tf_op jit(solution)/shard_map/ppermute | solution.py:299
  21.2 0.1 shard_map.106
  21.3 2.2 %collective-permute-start.5 = (bf16[96,256]{1,0:T(8,128)(2,1)S(1)}, bf16[96,256]{1,0:T(8,128)(2,1)S(1)}, u32[]{:S(2)}, u32[]{:S(2)}) collective-permute-start(bf16[96,256]{1,0:T(8,128)(2,1)S(1)} %get-tuple-element.31), channel_id=1, source_target_pairs={{0,6},{1,7},{2,4},{3,5},{4,2},{5,3},{6,0},{7,1},{8,14},{9,15},{10,... | collective-permute-start | bytes 147464 | tf_op jit(solution)/shard_map/ppermute | solution.py:299
  23.5 0.9 %collective-permute-start.6 = (bf16[96,256]{1,0:T(8,128)(2,1)S(1)}, bf16[96,256]{1,0:T(8,128)(2,1)S(1)}, u32[]{:S(2)}, u32[]{:S(2)}) collective-permute-start(bf16[96,256]{1,0:T(8,128)(2,1)S(1)} %get-tuple-element.32), channel_id=1, source_target_pairs={{0,4},{1,5},{2,6},{3,7},{4,0},{5,1},{6,2},{7,3},{8,12},{9,13},{10,... | collective-permute-start | bytes 147464 | tf_op jit(solution)/shard_map/ppermute | solution.py:299
  24.4 1.3 %collective-permute-start.7 = (bf16[96,256]{1,0:T(8,128)(2,1)S(1)}, bf16[96,256]{1,0:T(8,128)(2,1)S(1)}, u32[]{:S(2)}, u32[]{:S(2)}) collective-permute-start(bf16[96,256]{1,0:T(8,128)(2,1)S(1)} %get-tuple-element.33), channel_id=1, source_target_pairs={{0,2},{1,3},{2,0},{3,1},{4,6},{5,7},{6,4},{7,5},{8,10},{9,11},{10,... | collective-permute-start | bytes 147464 | tf_op jit(solution)/shard_map/ppermute | solution.py:299
  25.8 1.7 %collective-permute-done.5.refs_0_ = bf16[96,256]{1,0:T(8,128)(2,1)S(1)} collective-permute-done((bf16[96,256]{1,0:T(8,128)(2,1)S(1)}, bf16[96,256]{1,0:T(8,128)(2,1)S(1)}, u32[]{:S(2)}, u32[]{:S(2)}) %collective-permute-start.5) | collective-permute-done | bytes 49184 | tf_op jit(solution)/shard_map/ppermute | solution.py:299
  27.5 1.4 %collective-permute-done.6.refs_1_ = bf16[96,256]{1,0:T(8,128)(2,1)S(1)} collective-permute-done((bf16[96,256]{1,0:T(8,128)(2,1)S(1)}, bf16[96,256]{1,0:T(8,128)(2,1)S(1)}, u32[]{:S(2)}, u32[]{:S(2)}) %collective-permute-start.6) | collective-permute-done | bytes 49184 | tf_op jit(solution)/shard_map/ppermute | solution.py:299
  28.9 0.1 collective-permute-done.7.refs_2_
  29.1 0.1 shard_map.111.refs_1_
  29.2 0.0 copy-start.1
  29.2 0.0 copy-start.2
  29.2 0.1 collective-permute-start.13
  29.3 1.0 %collective-permute-start.14 = (bf16[96,256]{1,0:T(8,128)(2,1)S(1)}, bf16[96,256]{1,0:T(8,128)(2,1)S(1)}, u32[]{:S(2)}, u32[]{:S(2)}) collective-permute-start(bf16[96,256]{1,0:T(8,128)(2,1)S(1)} %shard_map.107.mine_ref.refs_5_.refs_3_), channel_id=1, source_target_pairs={{0,24},{8,16},{16,8},{24,0},{1,25},{9,17},{17,9},{25,1},{2,26},{10... | collective-permute-start | bytes 147464 | tf_op jit(solution)/shard_map/ppermute | solution.py:299
  30.2 1.2 %collective-permute-start.15 = (bf16[96,256]{1,0:T(8,128)(2,1)S(1)}, bf16[96,256]{1,0:T(8,128)(2,1)S(1)}, u32[]{:S(2)}, u32[]{:S(2)}) collective-permute-start(bf16[96,256]{1,0:T(8,128)(2,1)S(1)} %shard_map.107.mine_ref.refs_5_.refs_3_), channel_id=1, source_target_pairs={{0,16},{8,24},{16,0},{24,8},{1,17},{9,25},{17,1},{25,9},{2,18},{10... | collective-permute-start | bytes 147464 | tf_op jit(solution)/shard_map/ppermute | solution.py:299
  31.4 0.2 collective-permute-done.13.refs_2_.refs_4_
  31.6 1.3 %shard_map.112.refs_7_ = bf16[256,512]{1,0:T(8,128)(2,1)} custom-call(bf16[256,1536]{1,0:T(8,128)(2,1)S(1)} %get-tuple-element.21.normed_ref.refs_0_, bf16[1632,256]{1,0:T(8,128)(2,1)S(1)} %shard_map.111.refs_1_, bf16[1632,256]{1,0:T(8,128)(2,1)S(1)} %collective-permute-done.13.refs_2_.refs_4_, f32[256,128]{1,0:T(8,128)S(1)} %get-tuple-element.35.refs_3_, ...), custom_call_target="tpu_custom_call" | custom-call | bytes 1000000 | tf_op jit(solution)/shard_map/pallas_call | solution.py:92
  33.0 1.5 %collective-permute-done.15.refs_6_ = bf16[96,256]{1,0:T(8,128)(2,1)S(1)} collective-permute-done((bf16[96,256]{1,0:T(8,128)(2,1)S(1)}, bf16[96,256]{1,0:T(8,128)(2,1)S(1)}, u32[]{:S(2)}, u32[]{:S(2)}) %collective-permute-start.15) | collective-permute-done | bytes 49184 | tf_op jit(solution)/shard_map/ppermute | solution.py:299
  34.5 0.9 %shard_map.113 = (f32[192,512]{1,0:T(8,128)}, f32[192]{0:T(256)}) custom-call(s32[4,8]{1,0:T(4,128)S(1)} %copy-done.1, bf16[192]{0:T(256)(128)(2,1)S(1)} %copy-done.2, bf16[192,512]{1,0:T(8,128)(2,1)S(1)} %copy-done, bf16[96,256]{1,0:T(8,128)(2,1)S(1)} %shard_map.107.mine_ref.refs_5_.refs_3_, bf16[1632,256]{1,0:T(8,128)(2,1)S(1)} %collective-permute-done.13.refs_2_.refs_4_, ...), custom_call_target="tpu_custom_call" | custom-call | bytes 1000000 | tf_op jit(solution)/shard_map/pallas_call | solution.py:92
  (17 shorter events, 0.1 us)
Async XLA Ops:
  2.8 5.2 %collective-permute-start = (bf16[1152,256]{1,0:T(8,128)(2,1)S(1)}, bf16[1152,256]{1,0:T(8,128)(2,1)S(1)}, u32[]{:S(2)}, u32[]{:S(2)}) collective-permute-start(bf16[1152,256]{1,0:T(8,128)(2,1)S(1)} %get-tuple-element.24), channel_id=1, source_target_pairs={{0,8},{8,0},{1,9},{9,1},{2,10},{10,2},{3,11},{11,3},{4,12},{12,4},... | collective-permute-start | bytes 1769480 | tf_op jit(solution)/shard_map/ppermute | solution.py:299
  3.8 4.2 %collective-permute-start.1 = (bf16[384,256]{1,0:T(8,128)(2,1)S(1)}, bf16[384,256]{1,0:T(8,128)(2,1)S(1)}, u32[]{:S(2)}, u32[]{:S(2)}) collective-permute-start(bf16[384,256]{1,0:T(8,128)(2,1)S(1)} %get-tuple-element.25), channel_id=1, source_target_pairs={{0,8},{8,0},{1,9},{9,1},{2,10},{10,2},{3,11},{11,3},{4,12},{12,4},... | collective-permute-start | bytes 589832 | tf_op jit(solution)/shard_map/ppermute | solution.py:299
  4.0 9.3 %collective-permute-start.9 = (bf16[192,256]{1,0:T(8,128)(2,1)S(1)}, bf16[192,256]{1,0:T(8,128)(2,1)S(1)}, u32[]{:S(2)}, u32[]{:S(2)}) collective-permute-start(bf16[192,256]{1,0:T(8,128)(2,1)S(1)} %get-tuple-element.34.refs_0_), channel_id=1, source_target_pairs={{0,4},{1,5},{2,6},{3,7},{4,0},{5,1},{6,2},{7,3},{8,12},{9,13},{10,... | collective-permute-start | bytes 294920 | tf_op jit(solution)/shard_map/ppermute | solution.py:299
  8.1 11.7 %collective-permute-start.2 = (bf16[4,96,256]{2,1,0:T(8,128)(2,1)S(1)}, bf16[4,96,256]{2,1,0:T(8,128)(2,1)S(1)}, u32[]{:S(2)}, u32[]{:S(2)}) collective-permute-start(bf16[4,96,256]{2,1,0:T(8,128)(2,1)S(1)} %get-tuple-element.27), channel_id=1, source_target_pairs={{0,17},{1,16},{2,19},{3,18},{4,21},{5,20},{6,23},{7,22},{16,1},{17... | collective-permute-start | bytes 589832 | tf_op jit(solution)/shard_map/ppermute | solution.py:299
  10.6 10.6 %collective-permute-start.3 = (bf16[4,96,256]{2,1,0:T(8,128)(2,1)S(1)}, bf16[4,96,256]{2,1,0:T(8,128)(2,1)S(1)}, u32[]{:S(2)}, u32[]{:S(2)}) collective-permute-start(bf16[4,96,256]{2,1,0:T(8,128)(2,1)S(1)} %get-tuple-element.28), channel_id=1, source_target_pairs={{0,1},{1,0},{2,3},{3,2},{4,5},{5,4},{6,7},{7,6},{8,9},{9,8},{10,11... | collective-permute-start | bytes 589832 | tf_op jit(solution)/shard_map/ppermute | solution.py:299
  11.2 10.0 %collective-permute-start.4 = (bf16[4,96,256]{2,1,0:T(8,128)(2,1)S(1)}, bf16[4,96,256]{2,1,0:T(8,128)(2,1)S(1)}, u32[]{:S(2)}, u32[]{:S(2)}) collective-permute-start(bf16[4,96,256]{2,1,0:T(8,128)(2,1)S(1)} %get-tuple-element.29), channel_id=1, source_target_pairs={{0,16},{16,0},{1,17},{17,1},{2,18},{18,2},{3,19},{19,3},{4,20},{20... | collective-permute-start | bytes 589832 | tf_op jit(solution)/shard_map/ppermute | solution.py:299
  11.7 5.6 %collective-permute-start.8 = (bf16[192,256]{1,0:T(8,128)(2,1)S(1)}, bf16[192,256]{1,0:T(8,128)(2,1)S(1)}, u32[]{:S(2)}, u32[]{:S(2)}) collective-permute-start(bf16[192,256]{1,0:T(8,128)(2,1)S(1)} %get-tuple-element.34.refs_0_), channel_id=1, source_target_pairs={{0,2},{1,3},{2,0},{3,1},{4,6},{5,7},{6,4},{7,5},{8,10},{9,11},{10,... | collective-permute-start | bytes 294920 | tf_op jit(solution)/shard_map/ppermute | solution.py:299
  13.3 5.5 %collective-permute-start.10 = (bf16[192,256]{1,0:T(8,128)(2,1)S(1)}, bf16[192,256]{1,0:T(8,128)(2,1)S(1)}, u32[]{:S(2)}, u32[]{:S(2)}) collective-permute-start(bf16[192,256]{1,0:T(8,128)(2,1)S(1)} %bitcast.3), channel_id=1, source_target_pairs={{0,2},{1,3},{2,0},{3,1},{4,6},{5,7},{6,4},{7,5},{8,10},{9,11},{10,... | collective-permute-start | bytes 294920 | tf_op jit(solution)/shard_map/ppermute | solution.py:299
  17.3 11.8 %collective-permute-start.11 = (bf16[2,192,256]{2,1,0:T(8,128)(2,1)S(1)}, bf16[2,192,256]{2,1,0:T(8,128)(2,1)S(1)}, u32[]{:S(2)}, u32[]{:S(2)}) collective-permute-start(bf16[2,192,256]{2,1,0:T(8,128)(2,1)S(1)} %shard_map.108.refs_0_), channel_id=1, source_target_pairs={{0,1},{1,0},{2,3},{3,2},{4,5},{5,4},{6,7},{7,6},{8,9},{9,8},{10,11... | collective-permute-start | bytes 589832 | tf_op jit(solution)/shard_map/ppermute | solution.py:299
  18.8 10.3 %collective-permute-start.12 = (bf16[2,192,256]{2,1,0:T(8,128)(2,1)S(1)}, bf16[2,192,256]{2,1,0:T(8,128)(2,1)S(1)}, u32[]{:S(2)}, u32[]{:S(2)}) collective-permute-start(bf16[2,192,256]{2,1,0:T(8,128)(2,1)S(1)} %shard_map.110.refs_1_), channel_id=1, source_target_pairs={{0,1},{1,0},{2,3},{3,2},{4,5},{5,4},{6,7},{7,6},{8,9},{9,8},{10,11... | collective-permute-start | bytes 589832 | tf_op jit(solution)/shard_map/ppermute | solution.py:299
  21.3 6.2 %collective-permute-start.5 = (bf16[96,256]{1,0:T(8,128)(2,1)S(1)}, bf16[96,256]{1,0:T(8,128)(2,1)S(1)}, u32[]{:S(2)}, u32[]{:S(2)}) collective-permute-start(bf16[96,256]{1,0:T(8,128)(2,1)S(1)} %get-tuple-element.31), channel_id=1, source_target_pairs={{0,6},{1,7},{2,4},{3,5},{4,2},{5,3},{6,0},{7,1},{8,14},{9,15},{10,... | collective-permute-start | bytes 147464 | tf_op jit(solution)/shard_map/ppermute | solution.py:299
  23.5 5.3 %collective-permute-start.6 = (bf16[96,256]{1,0:T(8,128)(2,1)S(1)}, bf16[96,256]{1,0:T(8,128)(2,1)S(1)}, u32[]{:S(2)}, u32[]{:S(2)}) collective-permute-start(bf16[96,256]{1,0:T(8,128)(2,1)S(1)} %get-tuple-element.32), channel_id=1, source_target_pairs={{0,4},{1,5},{2,6},{3,7},{4,0},{5,1},{6,2},{7,3},{8,12},{9,13},{10,... | collective-permute-start | bytes 147464 | tf_op jit(solution)/shard_map/ppermute | solution.py:299
  24.4 4.6 %collective-permute-start.7 = (bf16[96,256]{1,0:T(8,128)(2,1)S(1)}, bf16[96,256]{1,0:T(8,128)(2,1)S(1)}, u32[]{:S(2)}, u32[]{:S(2)}) collective-permute-start(bf16[96,256]{1,0:T(8,128)(2,1)S(1)} %get-tuple-element.33), channel_id=1, source_target_pairs={{0,2},{1,3},{2,0},{3,1},{4,6},{5,7},{6,4},{7,5},{8,10},{9,11},{10,... | collective-permute-start | bytes 147464 | tf_op jit(solution)/shard_map/ppermute | solution.py:299
  29.2 5.3 %copy-start = (bf16[192,512]{1,0:T(8,128)(2,1)S(1)}, bf16[192,512]{1,0:T(8,128)(2,1)}, u32[]{:S(2)}) copy-start(bf16[192,512]{1,0:T(8,128)(2,1)} %refs_2_.1) | copy-start | bytes 589828
  29.2 5.3 %copy-start.1 = (s32[4,8]{1,0:T(4,128)S(1)}, s32[4,8]{1,0:T(4,128)}, u32[]{:S(2)}) copy-start(s32[4,8]{1,0:T(4,128)} %refs_0_.1) | copy-start | bytes 388
  29.2 5.3 %copy-start.2 = (bf16[192]{0:T(256)(128)(2,1)S(1)}, bf16[192]{0:T(256)(128)(2,1)}, u32[]{:S(2)}) copy-start(bf16[192]{0:T(256)(128)(2,1)} %refs_1_.1) | copy-start | bytes 1156
  29.2 2.4 %collective-permute-start.13 = (bf16[1632,256]{1,0:T(8,128)(2,1)S(1)}, bf16[1632,256]{1,0:T(8,128)(2,1)S(1)}, u32[]{:S(2)}, u32[]{:S(2)}) collective-permute-start(bf16[1632,256]{1,0:T(8,128)(2,1)S(1)} %shard_map.111.refs_1_), channel_id=1, source_target_pairs={{0,8},{8,0},{1,9},{9,1},{2,10},{10,2},{3,11},{11,3},{4,12},{12,4},... | collective-permute-start | bytes 2506760 | tf_op jit(solution)/shard_map/ppermute | solution.py:299
  29.3 3.7 %collective-permute-start.14 = (bf16[96,256]{1,0:T(8,128)(2,1)S(1)}, bf16[96,256]{1,0:T(8,128)(2,1)S(1)}, u32[]{:S(2)}, u32[]{:S(2)}) collective-permute-start(bf16[96,256]{1,0:T(8,128)(2,1)S(1)} %shard_map.107.mine_ref.refs_5_.refs_3_), channel_id=1, source_target_pairs={{0,24},{8,16},{16,8},{24,0},{1,25},{9,17},{17,9},{25,1},{2,26},{10... | collective-permute-start | bytes 147464 | tf_op jit(solution)/shard_map/ppermute | solution.py:299
  30.2 4.2 %collective-permute-start.15 = (bf16[96,256]{1,0:T(8,128)(2,1)S(1)}, bf16[96,256]{1,0:T(8,128)(2,1)S(1)}, u32[]{:S(2)}, u32[]{:S(2)}) collective-permute-start(bf16[96,256]{1,0:T(8,128)(2,1)S(1)} %shard_map.107.mine_ref.refs_5_.refs_3_), channel_id=1, source_target_pairs={{0,16},{8,24},{16,0},{24,8},{1,17},{9,25},{17,1},{25,9},{2,18},{10... | collective-permute-start | bytes 147464 | tf_op jit(solution)/shard_map/ppermute | solution.py:299
